TPU v7x, 256 devices: a whole 4x4x8 slice. The times are simulated.
256 devices in a mesh: row: 8 (over x_lo, y), col: 32 (over x_hi, z, core).
Axes of the slice: x: 4 (x_hi: 2, x_lo: 2; x = x_hi * 2 + x_lo), y: 4, z: 8, core: 2. Of those that a mesh axis runs over, the one named last changes fastest.
Arguments:
- tokens: bfloat16 [512, 12288], P('col', 'row'), may hold values from -6 to 6
- w_up: bfloat16 [12288, 24576], P('row', 'col'), may hold values from -0.0546875 to 0.0546875
- w_down: bfloat16 [24576, 12288], P('col', 'row'), may hold values from -0.0390625 to 0.0390625
- grad_out: bfloat16 [512, 12288], P('col', 'row'), may hold values from -6 to 6
Outputs:
- output: bfloat16 [512, 12288], P('col', 'row')
- grad_tokens: bfloat16 [512, 12288], P('col', 'row')
- grad_up: bfloat16 [12288, 24576], P('row', 'col')
- grad_down: bfloat16 [24576, 12288], P('col', 'row')
All inputs are finite; a program needn't handle non-finite values.
Results may differ from a plain program's by a relative error of at most 0.005.
Values may be sent and summed in bfloat16 or wider, within the bound.
No kernel may reach another device: no remote copies, remote signals or barrier semaphores. Data moves between devices by JAX's collectives and lax.ppermute only.
A program may use at most 64 MiB of HBM per device.

v0:
```python
import math

import jax
import jax.numpy as jnp
from jax import lax
from jax.sharding import PartitionSpec as P

gelu_coef = 0.7978845608028654


def activate(preact, back_grad):
    tanh_val = jnp.tanh(gelu_coef * (preact + 0.044715 * preact * preact * preact))
    activated = 0.5 * preact * (1.0 + tanh_val)
    derivative = 0.5 * (1.0 + tanh_val) + 0.5 * preact * (1.0 - tanh_val * tanh_val) * gelu_coef * (
        1.0 + 3.0 * 0.044715 * preact * preact
    )
    return (activated.astype(jnp.bfloat16), (back_grad * derivative).astype(jnp.bfloat16))


def local(tokens, w_up, w_down, grad_out):
    contract_last = (((1,), (1,)), ((), ()))
    contract_first = (((0,), (0,)), ((), ()))
    x_all, dy_all = (
        lax.all_gather(tokens, "col", axis=0, tiled=True),
        lax.all_gather(grad_out, "col", axis=0, tiled=True),
    )
    total_rows = x_all.shape[0]
    feat_width = w_up.shape[0]
    preact = jnp.dot(x_all, w_up, preferred_element_type=jnp.float32)
    back_grad = lax.dot_general(dy_all, w_down, contract_last, preferred_element_type=jnp.float32)
    preact, back_grad = lax.psum((preact, back_grad), "row")
    hidden, grad_pre = activate(preact, back_grad)
    grad_scale = 1.0 / math.sqrt(total_rows)
    grad_up = (
        lax.dot_general(x_all, grad_pre, contract_first, preferred_element_type=jnp.float32)
        * grad_scale
    ).astype(jnp.bfloat16)
    grad_down = (
        lax.dot_general(hidden, dy_all, contract_first, preferred_element_type=jnp.float32)
        * grad_scale
    ).astype(jnp.bfloat16)
    out_part = jnp.dot(hidden, w_down, preferred_element_type=jnp.float32)
    back_part = lax.dot_general(grad_pre, w_up, contract_last, preferred_element_type=jnp.float32)
    reduced = lax.psum_scatter(
        jnp.concatenate([out_part, back_part], axis=1), "col", scatter_dimension=0, tiled=True
    )
    output = reduced[:, :feat_width].astype(jnp.bfloat16)
    grad_tokens = reduced[:, feat_width:].astype(jnp.bfloat16)
    return (output, grad_tokens, grad_up, grad_down)


def solution(mesh):
    placed = (P("col", "row"), P("row", "col"), P("col", "row"), P("col", "row"))
    return jax.shard_map(
        local,
        mesh=mesh,
        in_specs=placed,
        out_specs=(P("col", "row"), P("col", "row"), P("row", "col"), P("col", "row")),
        check_vma=False,
    )
```

profile of v0, /device:TPU:8, one launch (start us, length us, event | category | flops | bytes accessed | tf_op | source)
XLA Modules:
  0.0 421.7 jit_solution(1165511677424131865)
XLA Ops:
  7.2 0.0 copy-start
  7.2 0.0 all-gather.5.cloned.1.call-start
  7.2 0.7 all-gather.5.cloned.1.call-update
  7.9 0.0 all-gather.3.cloned.1.call-start
  8.0 0.7 all-gather.3.cloned.1.call-update
  8.7 0.0 all-reduce.3.cloned.1.call-start
  8.7 83.7 %all-gather.5.cloned.1.call-done = bf16[512,1536]{1,0:T(8,128)(2,1)} async-done(((bf16[16,1536]{1,0:T(8,128)(2,1)}), bf16[512,1536]{1,0:T(8,128)(2,1)}) %all-gather.5.cloned.1.call-update) | async-done | bytes 1572880 | tf_op jit(solution)/shard_map/all_gather | solution.py:25
  92.4 0.0 copy-done
  92.4 4.0 fusion.11
  96.4 73.9 %all-gather.3.cloned.1.call-done = bf16[512,1536]{1,0:T(8,128)(2,1)} async-done(((bf16[16,1536]{1,0:T(8,128)(2,1)}), bf16[512,1536]{1,0:T(8,128)(2,1)}) %all-gather.3.cloned.1.call-update) | async-done | bytes 1572880 | tf_op jit(solution)/shard_map/all_gather | solution.py:24
  170.3 4.7 %fusion.10 = f32[512,768]{1,0:T(8,128)} fusion(bf16[512,1536]{1,0:T(8,128)(2,1)} %all-gather.3.cloned.1.call-done, bf16[1536,768]{1,0:T(8,128)(2,1)} %param.5), kind=kOutput, calls=%fused_computation.16 | convolution fusion | flops 1207959552 | bytes 5505024 | tf_op jit(solution)/shard_map/dot_general | solution.py:29
  175.0 0.0 all-reduce.3.cloned.1.call-update
  175.0 0.0 reduce-scatter.2.cloned.1.call-start
  175.1 91.1 %all-reduce.3.cloned.1.call-done = (f32[512,768]{1,0:T(8,128)}, f32[512,768]{1,0:T(8,128)}) async-done(((f32[512,768]{1,0:T(8,128)}, f32[512,768]{1,0:T(8,128)}), (f32[512,768]{1,0:T(8,128)}, f32[512,768]{1,0:T(8,128)})) %all-reduce.3.cloned.1.call-update) | async-done | bytes 3145744 | tf_op jit(solution)/shard_map/psum | solution.py:31
  266.1 0.0 copy-start.1
  266.1 0.0 copy-start.2
  266.1 3.0 fusion.8
  269.2 0.0 copy-done.1
  269.2 0.0 copy-done.2
  269.2 0.0 copy-start.3
  269.2 1.0 fusion.7
  270.2 0.6 copy-done.3
  270.9 1.4 fusion.12
  272.3 3.2 pad_maximum_fusion
  275.5 0.0 reduce-scatter.2.cloned.1.call-update
  275.5 4.2 %fusion = bf16[1536,768]{0,1:T(8,128)(2,1)} fusion(bf16[512,768]{1,0:T(8,128)(2,1)S(1)} %fusion.7, bf16[512,1536]{1,0:T(8,128)(2,1)} %all-gather.3.cloned.1.call-done), kind=kOutput, calls=%fused_computation.3 | convolution fusion | flops 1210318848 | bytes 4718592 | tf_op jit(solution)/shard_map/dot_general | solution.py:35
  279.7 4.3 %copy.8 = bf16[1536,768]{1,0:T(8,128)(2,1)} copy(bf16[1536,768]{0,1:T(8,128)(2,1)} %fusion) | data formatting | bytes 4718592
  284.0 4.8 %multiply_convert_fusion = bf16[768,1536]{1,0:T(8,128)(2,1)} fusion(bf16[512,1536]{1,0:T(8,128)(2,1)} %all-gather.5.cloned.1.call-done, f32[512,768]{1,0:T(8,128)} %get-tuple-element.9), kind=kOutput, calls=%fused_computation.1 | convolution fusion | flops 1213857792 | bytes 5505024 | tf_op jit(solution)/shard_map/dot_general | solution.py:39
  288.8 124.8 %reduce-scatter.2.cloned.1.call-done = f32[16,3072]{1,0:T(8,128)} async-done(((f32[512,3072]{1,0:T(8,128)}), f32[16,3072]{1,0:T(8,128)}) %reduce-scatter.2.cloned.1.call-update) | async-done | bytes 196624 | tf_op jit(solution)/shard_map/reduce_scatter | solution.py:44
  413.6 0.9 convert.4
  414.5 0.6 fusion.9
Async XLA Ops:
  7.2 85.3 %copy-start = (bf16[768,1536]{1,0:T(8,128)(2,1)S(1)}, bf16[768,1536]{1,0:T(8,128)(2,1)}, u32[]{:S(2)}) copy-start(bf16[768,1536]{1,0:T(8,128)(2,1)} %param.6) | copy-start | bytes 7077892
  7.2 85.2 %all-gather.5.cloned.1.call-start = ((), (), s32[]{:S(2)}) async-start(), calls=%async_computation.2 | async-start | bytes 1622016 | tf_op jit(solution)/shard_map/all_gather | solution.py:25
  7.9 162.4 %all-gather.3.cloned.1.call-start = ((), (), s32[]{:S(2)}) async-start(), calls=%async_computation.1 | async-start | bytes 1622016 | tf_op jit(solution)/shard_map/all_gather | solution.py:24
  8.7 257.5 %all-reduce.3.cloned.1.call-start = ((), (), s32[]{:S(2)}) async-start(), calls=%async_computation.4 | async-start | bytes 6291456 | tf_op jit(solution)/shard_map/psum | solution.py:31
  175.0 238.6 %reduce-scatter.2.cloned.1.call-start = ((), (), s32[]{:S(2)}) async-start(), calls=%async_computation.3 | async-start | bytes 6488064 | tf_op jit(solution)/shard_map/reduce_scatter | solution.py:44
  266.1 3.0 copy-start.1
  266.1 3.0 copy-start.2
  269.2 1.7 copy-start.3
Sparse Core Ops, SparseCore 0:
  10.8 81.5 all-gather.4
  95.2 75.0 all-gather.2
  175.1 90.9 all-reduce.2
  275.6 137.9 reduce-scatter.1
where the time goes:
time: 422 us
  waiting for transfers between devices  375 us (89%)
  matrix products  22.1 us (5%)
  between operations  13.8 us (3%)
  local copies, waits for them, and re-layouts  5.58 us (1%)
  other arithmetic  5.15 us (1%)
    reduce_scatter x1, waiting for transfers between devices, local(): lax.psum_scatter(jnp.concatenate([out_part, back_part], axis=1), 'col', s...  125 us
    psum x1, waiting for transfers between devices, local(): preact, back_grad = lax.psum((preact, back_grad), 'row')  91.1 us
    all_gather x1, waiting for transfers between devices, local(): lax.all_gather(grad_out, 'col', axis=0, tiled=True)  83.7 us
    all_gather x1, waiting for transfers between devices, local(): lax.all_gather(tokens, 'col', axis=0, tiled=True)  73.9 us
  transfers between devices with their start and end apart: 4, of which 4 were waited for; matrix products, arithmetic and copies ran while one was open for 4% of the time, Pallas kernels for 0%

commit v1 on v0

v1 whole, which is shorter than its diff:
```python
import math

import jax
import jax.numpy as jnp
from jax import lax
from jax.sharding import PartitionSpec as P

gelu_coef = 0.7978845608028654


def activate(preact, back_grad):
    tanh_val = jnp.tanh(gelu_coef * (preact + 0.044715 * preact * preact * preact))
    activated = 0.5 * preact * (1.0 + tanh_val)
    derivative = 0.5 * (1.0 + tanh_val) + 0.5 * preact * (1.0 - tanh_val * tanh_val) * gelu_coef * (
        1.0 + 3.0 * 0.044715 * preact * preact
    )
    return (activated.astype(jnp.bfloat16), (back_grad * derivative).astype(jnp.bfloat16))


def perms(cols):
    ring = cols // 4

    def index(x_hi, z, core):
        return (x_hi * ring + z % ring) * 2 + core

    places = [(h, z, c) for h in range(2) for z in range(ring) for c in range(2)]
    swap_core = [(index(h, z, c), index(h, z, 1 - c)) for h, z, c in places]
    swap_half = [(index(h, z, c), index(1 - h, z, c)) for h, z, c in places]

    def pairing(phase):
        def partner(z, c):
            return z + 1 if (z + c + phase) % 2 == 0 else z - 1

        return [(index(h, z, c), index(h, partner(z, c), c)) for h, z, c in places]

    return swap_core, swap_half, pairing(0), pairing(1)


def local(swap_core, swap_half, even, odd, rows, tokens, w_up, w_down, grad_out):
    contract_last = (((1,), (1,)), ((), ()))
    contract_first = (((0,), (0,)), ((), ()))

    def swap(value, perm):
        return lax.ppermute(value, "col", perm)

    share = tokens.shape[0]
    feats = tokens.shape[1]
    total_rows = share * len(swap_core)
    hid = w_up.shape[1]
    grad_scale = 1.0 / math.sqrt(total_rows)

    mine = jnp.concatenate([tokens, grad_out], axis=1)
    unit = jnp.concatenate([mine, swap(mine, swap_half)], axis=0)
    first = jnp.concatenate([unit, swap(unit, even)], axis=0)
    second = swap(first, odd)
    third = swap(second, even)
    fourth = swap(third, odd)
    w_up_all = jnp.concatenate([w_up, swap(w_up, swap_core)], axis=1)
    w_down_all = jnp.concatenate([w_down, swap(w_down, swap_core)], axis=0)
    both = jnp.concatenate([first, second, third, fourth], axis=0)
    x_own, dy_own = both[:, :feats], both[:, feats:]
    units = both.shape[0] // rows

    preact = jnp.dot(x_own, w_up_all, preferred_element_type=jnp.float32).astype(jnp.bfloat16)
    back_grad = lax.dot_general(
        dy_own, w_down_all, contract_last, preferred_element_type=jnp.float32
    ).astype(jnp.bfloat16)
    parts = jnp.stack(
        [preact.reshape(rows, units, 2 * hid), back_grad.reshape(rows, units, 2 * hid)], axis=1
    )
    parts = lax.all_to_all(parts, "row", 0, 0)
    sums = jnp.sum(parts.astype(jnp.float32), axis=0)
    hidden, grad_pre = activate(sums[0], sums[1])
    pair = jnp.stack([hidden, grad_pre])
    spread = lax.all_to_all(jnp.broadcast_to(pair[None], (rows,) + pair.shape), "row", 0, 0)
    hidden = spread[:, 0].reshape(rows * units, 2 * hid)
    grad_pre = spread[:, 1].reshape(rows * units, 2 * hid)

    out_part = jnp.dot(hidden, w_down_all, preferred_element_type=jnp.float32)
    back_part = lax.dot_general(
        grad_pre, w_up_all, contract_last, preferred_element_type=jnp.float32
    )
    part = jnp.concatenate([out_part, back_part], axis=1)
    held = first.shape[0]
    blocks = [part[i * held : (i + 1) * held] for i in range(4)]

    def add(value, sent, perm):
        return value + swap(sent.astype(jnp.bfloat16), perm).astype(jnp.float32)

    acc = add(blocks[2], blocks[3], odd)
    acc = add(blocks[1], acc, even)
    acc = add(blocks[0], acc, odd)
    acc = add(acc[: held // 2], acc[held // 2 :], even)
    acc = add(acc[:share], acc[share:], swap_half)
    output = acc[:, :feats].astype(jnp.bfloat16)
    grad_tokens = acc[:, feats:].astype(jnp.bfloat16)

    both_other = swap(both, swap_core)
    acts_other = swap(jnp.stack([hidden[:, hid:], grad_pre[:, hid:]]), swap_core)
    both_all = jnp.concatenate([both, both_other], axis=0)
    hidden_all = jnp.concatenate([hidden[:, :hid], acts_other[0]], axis=0)
    grad_pre_all = jnp.concatenate([grad_pre[:, :hid], acts_other[1]], axis=0)
    grad_up = (
        lax.dot_general(
            both_all[:, :feats], grad_pre_all, contract_first, preferred_element_type=jnp.float32
        )
        * grad_scale
    ).astype(jnp.bfloat16)
    grad_down = (
        lax.dot_general(
            hidden_all, both_all[:, feats:], contract_first, preferred_element_type=jnp.float32
        )
        * grad_scale
    ).astype(jnp.bfloat16)
    return (output, grad_tokens, grad_up, grad_down)


def solution(mesh):
    placed = (P("col", "row"), P("row", "col"), P("col", "row"), P("col", "row"))
    rows, cols = mesh.shape["row"], mesh.shape["col"]
    swaps = perms(cols)

    def block(*args):
        return local(*swaps, rows, *args)

    return jax.shard_map(
        block,
        mesh=mesh,
        in_specs=placed,
        out_specs=(P("col", "row"), P("col", "row"), P("row", "col"), P("col", "row")),
        check_vma=False,
    )
```

time: 422 us -> 137 us (0.32)
  waiting for transfers between devices: 375 us -> 51.5 us
  blocking collectives: 0 us -> 37.5 us
  starting transfers between devices: 0.16 us -> 28.7 us
  between operations: 13.8 us -> 0.91 us
  matrix products: 22.1 us -> 11.3 us
    all_gather x2 -> x0, waiting for transfers between devices: 158 us -> none  [the longest x1 83.7 us: local(): lax.all_gather(grad_out, 'col', axis=0, tiled=True)]
    reduce_scatter x1 -> x0, waiting for transfers between devices: 125 us -> none  [local(): lax.psum_scatter(jnp.concatenate([out_part, back_part], axis=1), 'col', s...]
    psum x1 -> x0, waiting for transfers between devices: 91.1 us -> none  [local(): preact, back_grad = lax.psum((preact, back_grad), 'row')]
    ppermute x0 -> x14, waiting for transfers between devices: none -> 51.5 us  [swap(): return lax.ppermute(value, 'col', perm)]
    all_to_all x0 -> x2, blocking collectives: none -> 37.5 us  [the longest x1 19.7 us: local(): parts = lax.all_to_all(parts, 'row', 0, 0)]
    ppermute x0 -> x14, starting transfers between devices: none -> 28.7 us  [swap(): return lax.ppermute(value, 'col', perm)]
    dot_general x6, matrix products: 22.1 us -> 11.3 us  [the longest x1 2.85 us: local(): lax.dot_general(both_all[:, :feats], grad_pre_all, contract_first, prefer...]
  transfers between devices with their start and end apart: 4 -> 14, of which waited for: 4 -> 10; matrix products, arithmetic and copies ran while one was open for 4% -> 7% of each run, Pallas kernels for 0% -> 0%
where the time goes in v1:
time: 137 us; the launch traced here: 136 us
  waiting for transfers between devices  51.5 us (38%)
  blocking collectives  37.5 us (27%)
  starting transfers between devices  28.7 us (21%)
  matrix products  11.3 us (8%)
  local copies, waits for them, and re-layouts  5.39 us (4%)
    ppermute x14, waiting for transfers between devices, swap(): return lax.ppermute(value, 'col', perm)  51.5 us
    ppermute x14, starting transfers between devices, swap(): return lax.ppermute(value, 'col', perm)  28.7 us
    all_to_all x1, blocking collectives, local(): parts = lax.all_to_all(parts, 'row', 0, 0)  19.7 us
    all_to_all x1, blocking collectives, local(): lax.all_to_all(jnp.broadcast_to(pair[None], (rows,) + pair.shape), 'row',...  17.8 us
    unnamed x11, local copies, waits for them, and re-layouts  3.88 us
    dot_general x1, matrix products, local(): lax.dot_general(both_all[:, :feats], grad_pre_all, contract_first, prefer...  2.85 us
    dot_general x1, matrix products, local(): lax.dot_general(hidden_all, both_all[:, feats:], contract_first, preferre...  2.83 us
  transfers between devices with their start and end apart: 14, of which 10 were waited for; matrix products, arithmetic and copies ran while one was open for 7% of the time, Pallas kernels for 0%

profile of v1, /device:TPU:8, one launch (start us, length us, event | category | flops | bytes accessed | tf_op | source)
XLA Modules:
  0.0 136.3 jit_solution(11946456894431355701)
XLA Ops:
  0.6 0.8 constant_dynamic-update-slice_fusion.20
  1.4 0.8 constant_dynamic-update-slice_fusion.19
  2.3 3.1 %collective-permute-start = (bf16[16,3072]{1,0:T(8,128)(2,1)S(1)}, bf16[16,3072]{1,0:T(8,128)(2,1)S(1)}, u32[]{:S(2)}, u32[]{:S(2)}) collective-permute-start(bf16[16,3072]{1,0:T(8,128)(2,1)S(1)} %get-tuple-element.28), channel_id=1, source_target_pairs={{0,16},{1,17},{2,18},{3,19},{4,20},{5,21},{6,22},{7,23},{8,24},{9,... | collective-permute-start | bytes 294920 | tf_op jit(solution)/shard_map/ppermute | solution.py:44
  5.4 3.1 %collective-permute-done = bf16[16,3072]{1,0:T(8,128)(2,1)S(1)} collective-permute-done((bf16[16,3072]{1,0:T(8,128)(2,1)S(1)}, bf16[16,3072]{1,0:T(8,128)(2,1)S(1)}, u32[]{:S(2)}, u32[]{:S(2)}) %collective-permute-start) | collective-permute-done | bytes 98336 | tf_op jit(solution)/shard_map/ppermute | solution.py:44
  8.5 2.0 %collective-permute-start.1 = (bf16[32,3072]{1,0:T(8,128)(2,1)S(1)}, bf16[32,3072]{1,0:T(8,128)(2,1)S(1)}, u32[]{:S(2)}, u32[]{:S(2)}) collective-permute-start(bf16[32,3072]{1,0:T(8,128)(2,1)S(1)} %pad_maximum_fusion.4), channel_id=1, source_target_pairs={{0,2},{1,15},{2,0},{3,5},{4,6},{5,3},{6,4},{7,9},{8,10},{9,7},{10,... | collective-permute-start | bytes 589832 | tf_op jit(solution)/shard_map/ppermute | solution.py:44
  10.5 2.3 %collective-permute-start.5 = (bf16[1536,768]{1,0:T(8,128)(2,1)}, bf16[1536,768]{1,0:T(8,128)(2,1)S(1)}, u32[]{:S(2)}, u32[]{:S(2)}) collective-permute-start(bf16[1536,768]{1,0:T(8,128)(2,1)} %param.5), channel_id=1, source_target_pairs={{0,1},{1,0},{2,3},{3,2},{4,5},{5,4},{6,7},{7,6},{8,9},{9,8},{10,11... | collective-permute-start | bytes 7077896 | tf_op jit(solution)/shard_map/ppermute | solution.py:44
  12.8 0.0 collective-permute-start.6
  12.8 1.4 %collective-permute-done.1 = bf16[32,3072]{1,0:T(8,128)(2,1)S(1)} collective-permute-done((bf16[32,3072]{1,0:T(8,128)(2,1)S(1)}, bf16[32,3072]{1,0:T(8,128)(2,1)S(1)}, u32[]{:S(2)}, u32[]{:S(2)}) %collective-permute-start.1) | collective-permute-done | bytes 196640 | tf_op jit(solution)/shard_map/ppermute | solution.py:44
  14.3 0.0 copy-start
  14.3 5.9 %collective-permute-start.2 = (bf16[64,3072]{1,0:T(8,128)(2,1)S(1)}, bf16[64,3072]{1,0:T(8,128)(2,1)S(1)}, u32[]{:S(2)}, u32[]{:S(2)}) collective-permute-start(bf16[64,3072]{1,0:T(8,128)(2,1)S(1)} %pad_maximum_fusion.3), channel_id=1, source_target_pairs={{0,14},{1,3},{2,4},{3,1},{4,2},{5,7},{6,8},{7,5},{8,6},{9,11},{10,... | collective-permute-start | bytes 1179656 | tf_op jit(solution)/shard_map/ppermute | solution.py:44
  20.2 1.8 %constant_dynamic-update-slice_fusion.10 = bf16[1536,1536]{1,0:T(8,128)(2,1)S(1)} fusion(bf16[1536,768]{1,0:T(8,128)(2,1)} %param.5), kind=kLoop, calls=%fused_computation.65 | loop fusion | bytes 4718592
  22.1 0.0 copy-done
  22.1 0.2 constant_dynamic-update-slice_fusion.12
  22.2 3.7 %collective-permute-done.2 = bf16[64,3072]{1,0:T(8,128)(2,1)S(1)} collective-permute-done((bf16[64,3072]{1,0:T(8,128)(2,1)S(1)}, bf16[64,3072]{1,0:T(8,128)(2,1)S(1)}, u32[]{:S(2)}, u32[]{:S(2)}) %collective-permute-start.2) | collective-permute-done | bytes 393248 | tf_op jit(solution)/shard_map/ppermute | solution.py:44
  26.0 0.0 collective-permute-start.3
  26.0 8.0 %collective-permute-done.3 = bf16[64,3072]{1,0:T(8,128)(2,1)S(1)} collective-permute-done((bf16[64,3072]{1,0:T(8,128)(2,1)S(1)}, bf16[64,3072]{1,0:T(8,128)(2,1)S(1)}, u32[]{:S(2)}, u32[]{:S(2)}) %collective-permute-start.3) | collective-permute-done | bytes 393248 | tf_op jit(solution)/shard_map/ppermute | solution.py:44
  34.1 3.5 %collective-permute-start.4 = (bf16[64,3072]{1,0:T(8,128)(2,1)S(1)}, bf16[64,3072]{1,0:T(8,128)(2,1)S(1)}, u32[]{:S(2)}, u32[]{:S(2)}) collective-permute-start(bf16[64,3072]{1,0:T(8,128)(2,1)S(1)} %collective-permute-done.3), channel_id=1, source_target_pairs={{0,14},{1,3},{2,4},{3,1},{4,2},{5,7},{6,8},{7,5},{8,6},{9,11},{10,... | collective-permute-start | bytes 1179656 | tf_op jit(solution)/shard_map/ppermute | solution.py:44
  37.6 0.1 constant_dynamic-update-slice_fusion.16
  37.7 0.1 constant_dynamic-update-slice_fusion.15
  37.7 5.6 %collective-permute-done.4 = bf16[64,3072]{1,0:T(8,128)(2,1)S(1)} collective-permute-done((bf16[64,3072]{1,0:T(8,128)(2,1)S(1)}, bf16[64,3072]{1,0:T(8,128)(2,1)S(1)}, u32[]{:S(2)}, u32[]{:S(2)}) %collective-permute-start.4) | collective-permute-done | bytes 393248 | tf_op jit(solution)/shard_map/ppermute | solution.py:44
  43.3 0.1 constant_dynamic-update-slice_fusion.14
  43.4 0.0 collective-permute-done.6
  43.4 0.2 constant_dynamic-update-slice_fusion.11
  43.6 1.4 %convolution_convert_fusion = bf16[256,1536]{1,0:T(8,128)(2,1)S(1)} fusion(bf16[1536,1536]{1,0:T(8,128)(2,1)S(1)} %constant_dynamic-update-slice_fusion.11, bf16[256,3072]{1,0:T(8,128)(2,1)S(1)} %get-tuple-element.13), kind=kOutput, calls=%fused_computation.9 | convolution fusion | flops 1208352768 | bytes 6291456 | tf_op jit(solution)/shard_map/dot_general | solution.py:65
  45.0 0.0 collective-permute-done.5
  45.0 0.2 constant_dynamic-update-slice_fusion.9
  45.2 1.4 %convolution_convert_fusion.1 = bf16[256,1536]{1,0:T(8,128)(2,1)S(1)} fusion(bf16[1536,1536]{1,0:T(8,128)(2,1)S(1)} %constant_dynamic-update-slice_fusion.9, bf16[256,3072]{1,0:T(8,128)(2,1)S(1)} %get-tuple-element.13), kind=kOutput, calls=%fused_computation.10 | convolution fusion | flops 1208352768 | bytes 6291456 | tf_op jit(solution)/shard_map/dot_general | solution.py:64
  46.6 0.2 pad_maximum_fusion
  46.7 19.7 %all_to_all.10 = bf16[8,2,32,1536]{3,2,1,0:T(8,128)(2,1)S(1)} all-to-all(bf16[8,2,32,1536]{3,2,1,0:T(8,128)(2,1)S(1)} %pad_maximum_fusion), channel_id=1, replica_groups=mesh['row'=8,'col'=32] {'row'}, dimensions={0} | all-to-all | bytes 3145728 | tf_op jit(solution)/shard_map/all_to_all | solution.py:71
  66.5 0.2 convert_reduce_fusion
  66.7 0.1 multiply_convert_fusion.2
  66.9 0.1 broadcast_in_dim.2
  67.0 17.8 %all_to_all.11 = bf16[8,2,32,1536]{3,2,1,0:T(8,128)(2,1)S(1)} all-to-all(bf16[8,2,32,1536]{3,2,1,0:T(8,128)(2,1)S(1)} %broadcast_in_dim.2), channel_id=1, replica_groups=mesh['row'=8,'col'=32] {'row'}, dimensions={0} | all-to-all | bytes 3145728 | tf_op jit(solution)/shard_map/all_to_all | solution.py:75
  84.8 0.1 fusion.29
  84.9 1.4 %fusion.34 = f32[256,1536]{1,0:T(8,128)S(1)} fusion(bf16[256,1536]{1,0:T(8,128)(2,1)S(1)} %bitcast.22, bf16[1536,1536]{1,0:T(8,128)(2,1)S(1)} %constant_dynamic-update-slice_fusion.9), kind=kOutput, calls=%fused_computation.83 | convolution fusion | flops 1207959552 | bytes 7077888 | tf_op jit(solution)/shard_map/dot_general | solution.py:80
  86.4 1.4 %fusion.33 = f32[256,1536]{1,0:T(8,128)S(1)} fusion(bf16[256,1536]{1,0:T(8,128)(2,1)S(1)} %bitcast.24, bf16[1536,1536]{1,0:T(8,128)(2,1)S(1)} %constant_dynamic-update-slice_fusion.11), kind=kOutput, calls=%fused_computation.82 | convolution fusion | flops 1207959552 | bytes 7077888 | tf_op jit(solution)/shard_map/dot_general | solution.py:79
  87.8 3.3 %collective-permute-start.7 = (bf16[64,3072]{1,0:T(8,128)(2,1)S(1)}, bf16[64,3072]{1,0:T(8,128)(2,1)S(1)}, u32[]{:S(2)}, u32[]{:S(2)}) collective-permute-start(bf16[64,3072]{1,0:T(8,128)(2,1)S(1)} %fusion.10), channel_id=1, source_target_pairs={{0,14},{1,3},{2,4},{3,1},{4,2},{5,7},{6,8},{7,5},{8,6},{9,11},{10,... | collective-permute-start | bytes 1179656 | tf_op jit(solution)/shard_map/ppermute | solution.py:44
  91.1 0.0 collective-permute-start.12
  91.1 9.3 %collective-permute-done.7 = bf16[64,3072]{1,0:T(8,128)(2,1)S(1)} collective-permute-done((bf16[64,3072]{1,0:T(8,128)(2,1)S(1)}, bf16[64,3072]{1,0:T(8,128)(2,1)S(1)}, u32[]{:S(2)}, u32[]{:S(2)}) %collective-permute-start.7) | collective-permute-done | bytes 393248 | tf_op jit(solution)/shard_map/ppermute | solution.py:44
  100.5 0.1 fusion.4
  100.5 1.0 collective-permute-start.8
  101.6 0.1 fusion.30
  101.7 0.1 pad_maximum_fusion.2
  101.8 0.3 collective-permute-start.13
  102.0 9.4 %collective-permute-done.8 = bf16[64,3072]{1,0:T(8,128)(2,1)S(1)} collective-permute-done((bf16[64,3072]{1,0:T(8,128)(2,1)S(1)}, bf16[64,3072]{1,0:T(8,128)(2,1)S(1)}, u32[]{:S(2)}, u32[]{:S(2)}) %collective-permute-start.8) | collective-permute-done | bytes 393248 | tf_op jit(solution)/shard_map/ppermute | solution.py:44
  111.5 0.1 fusion.9
  111.6 4.2 %collective-permute-start.9 = (bf16[64,3072]{1,0:T(8,128)(2,1)S(1)}, bf16[64,3072]{1,0:T(8,128)(2,1)S(1)}, u32[]{:S(2)}, u32[]{:S(2)}) collective-permute-start(bf16[64,3072]{1,0:T(8,128)(2,1)S(1)} %fusion.9), channel_id=1, source_target_pairs={{0,14},{1,3},{2,4},{3,1},{4,2},{5,7},{6,8},{7,5},{8,6},{9,11},{10,... | collective-permute-start | bytes 1179656 | tf_op jit(solution)/shard_map/ppermute | solution.py:44
  115.7 0.0 collective-permute-done.12
  115.7 0.1 constant_dynamic-update-slice_fusion.13
  115.8 0.0 collective-permute-done.13
  115.9 0.1 slice_bitcast_fusion
  115.9 7.6 %collective-permute-done.9 = bf16[64,3072]{1,0:T(8,128)(2,1)S(1)} collective-permute-done((bf16[64,3072]{1,0:T(8,128)(2,1)S(1)}, bf16[64,3072]{1,0:T(8,128)(2,1)S(1)}, u32[]{:S(2)}, u32[]{:S(2)}) %collective-permute-start.9) | collective-permute-done | bytes 393248 | tf_op jit(solution)/shard_map/ppermute | solution.py:44
  123.5 0.1 fusion.6
  123.6 0.1 collective-permute-start.10
  123.7 2.9 %multiply_convert_fusion.1 = bf16[1536,768]{1,0:T(8,128)(2,1)} fusion(bf16[512,3072]{1,0:T(8,128)(2,1)S(1)} %constant_dynamic-update-slice_fusion.13, bf16[256,768]{1,0:T(8,128)(2,1)S(1)} %get-tuple-element.9, bf16[256,768]{1,0:T(8,128)(2,1)S(1)} %get-tuple-element.33), kind=kOutput, calls=%fused_computation.1 | convolution fusion | flops 1211891712 | bytes 4718592 | tf_op jit(solution)/shard_map/dot_general | solution.py:104
  126.6 2.8 %collective-permute-done.10 = bf16[32,3072]{1,0:T(8,128)(2,1)S(1)} collective-permute-done((bf16[32,3072]{1,0:T(8,128)(2,1)S(1)}, bf16[32,3072]{1,0:T(8,128)(2,1)S(1)}, u32[]{:S(2)}, u32[]{:S(2)}) %collective-permute-start.10) | collective-permute-done | bytes 196640 | tf_op jit(solution)/shard_map/ppermute | solution.py:44
  129.4 2.9 %collective-permute-start.11 = (bf16[16,3072]{1,0:T(8,128)(2,1)S(1)}, bf16[16,3072]{1,0:T(8,128)(2,1)S(1)}, u32[]{:S(2)}, u32[]{:S(2)}) collective-permute-start(bf16[16,3072]{1,0:T(8,128)(2,1)S(1)} %slice.182), channel_id=1, source_target_pairs={{0,16},{1,17},{2,18},{3,19},{4,20},{5,21},{6,22},{7,23},{8,24},{9,... | collective-permute-start | bytes 294920 | tf_op jit(solution)/shard_map/ppermute | solution.py:44
  132.4 2.8 %multiply_convert_fusion = bf16[768,1536]{1,0:T(8,128)(2,1)} fusion(bf16[512,3072]{1,0:T(8,128)(2,1)S(1)} %constant_dynamic-update-slice_fusion.13, bf16[256,768]{1,0:T(8,128)(2,1)S(1)} %get-tuple-element.8, bf16[256,768]{1,0:T(8,128)(2,1)S(1)} %get-tuple-element.6), kind=kOutput, calls=%fused_computation | convolution fusion | flops 1211891712 | bytes 4718592 | tf_op jit(solution)/shard_map/dot_general | solution.py:110
  135.2 0.4 collective-permute-done.11
  135.7 0.6 fusion.32
  (10 shorter events, 0.2 us)
Async XLA Ops:
  2.3 6.2 %collective-permute-start = (bf16[16,3072]{1,0:T(8,128)(2,1)S(1)}, bf16[16,3072]{1,0:T(8,128)(2,1)S(1)}, u32[]{:S(2)}, u32[]{:S(2)}) collective-permute-start(bf16[16,3072]{1,0:T(8,128)(2,1)S(1)} %get-tuple-element.28), channel_id=1, source_target_pairs={{0,16},{1,17},{2,18},{3,19},{4,20},{5,21},{6,22},{7,23},{8,24},{9,... | collective-permute-start | bytes 294920 | tf_op jit(solution)/shard_map/ppermute | solution.py:44
  8.5 5.8 %collective-permute-start.1 = (bf16[32,3072]{1,0:T(8,128)(2,1)S(1)}, bf16[32,3072]{1,0:T(8,128)(2,1)S(1)}, u32[]{:S(2)}, u32[]{:S(2)}) collective-permute-start(bf16[32,3072]{1,0:T(8,128)(2,1)S(1)} %pad_maximum_fusion.4), channel_id=1, source_target_pairs={{0,2},{1,15},{2,0},{3,5},{4,6},{5,3},{6,4},{7,9},{8,10},{9,7},{10,... | collective-permute-start | bytes 589832 | tf_op jit(solution)/shard_map/ppermute | solution.py:44
  10.5 34.5 %collective-permute-start.5 = (bf16[1536,768]{1,0:T(8,128)(2,1)}, bf16[1536,768]{1,0:T(8,128)(2,1)S(1)}, u32[]{:S(2)}, u32[]{:S(2)}) collective-permute-start(bf16[1536,768]{1,0:T(8,128)(2,1)} %param.5), channel_id=1, source_target_pairs={{0,1},{1,0},{2,3},{3,2},{4,5},{5,4},{6,7},{7,6},{8,9},{9,8},{10,11... | collective-permute-start | bytes 7077896 | tf_op jit(solution)/shard_map/ppermute | solution.py:44
  12.8 30.6 %collective-permute-start.6 = (bf16[768,1536]{1,0:T(8,128)(2,1)}, bf16[768,1536]{1,0:T(8,128)(2,1)S(1)}, u32[]{:S(2)}, u32[]{:S(2)}) collective-permute-start(bf16[768,1536]{1,0:T(8,128)(2,1)} %param.6), channel_id=1, source_target_pairs={{0,1},{1,0},{2,3},{3,2},{4,5},{5,4},{6,7},{7,6},{8,9},{9,8},{10,11... | collective-permute-start | bytes 7077896 | tf_op jit(solution)/shard_map/ppermute | solution.py:44
  14.3 7.8 %copy-start = (bf16[768,1536]{1,0:T(8,128)(2,1)S(1)}, bf16[768,1536]{1,0:T(8,128)(2,1)}, u32[]{:S(2)}) copy-start(bf16[768,1536]{1,0:T(8,128)(2,1)} %param.6) | copy-start | bytes 7077892
  14.3 11.7 %collective-permute-start.2 = (bf16[64,3072]{1,0:T(8,128)(2,1)S(1)}, bf16[64,3072]{1,0:T(8,128)(2,1)S(1)}, u32[]{:S(2)}, u32[]{:S(2)}) collective-permute-start(bf16[64,3072]{1,0:T(8,128)(2,1)S(1)} %pad_maximum_fusion.3), channel_id=1, source_target_pairs={{0,14},{1,3},{2,4},{3,1},{4,2},{5,7},{6,8},{7,5},{8,6},{9,11},{10,... | collective-permute-start | bytes 1179656 | tf_op jit(solution)/shard_map/ppermute | solution.py:44
  26.0 8.1 %collective-permute-start.3 = (bf16[64,3072]{1,0:T(8,128)(2,1)S(1)}, bf16[64,3072]{1,0:T(8,128)(2,1)S(1)}, u32[]{:S(2)}, u32[]{:S(2)}) collective-permute-start(bf16[64,3072]{1,0:T(8,128)(2,1)S(1)} %collective-permute-done.2), channel_id=1, source_target_pairs={{0,2},{1,15},{2,0},{3,5},{4,6},{5,3},{6,4},{7,9},{8,10},{9,7},{10,... | collective-permute-start | bytes 1179656 | tf_op jit(solution)/shard_map/ppermute | solution.py:44
  34.1 9.3 %collective-permute-start.4 = (bf16[64,3072]{1,0:T(8,128)(2,1)S(1)}, bf16[64,3072]{1,0:T(8,128)(2,1)S(1)}, u32[]{:S(2)}, u32[]{:S(2)}) collective-permute-start(bf16[64,3072]{1,0:T(8,128)(2,1)S(1)} %collective-permute-done.3), channel_id=1, source_target_pairs={{0,14},{1,3},{2,4},{3,1},{4,2},{5,7},{6,8},{7,5},{8,6},{9,11},{10,... | collective-permute-start | bytes 1179656 | tf_op jit(solution)/shard_map/ppermute | solution.py:44
  87.8 12.7 %collective-permute-start.7 = (bf16[64,3072]{1,0:T(8,128)(2,1)S(1)}, bf16[64,3072]{1,0:T(8,128)(2,1)S(1)}, u32[]{:S(2)}, u32[]{:S(2)}) collective-permute-start(bf16[64,3072]{1,0:T(8,128)(2,1)S(1)} %fusion.10), channel_id=1, source_target_pairs={{0,14},{1,3},{2,4},{3,1},{4,2},{5,7},{6,8},{7,5},{8,6},{9,11},{10,... | collective-permute-start | bytes 1179656 | tf_op jit(solution)/shard_map/ppermute | solution.py:44
  91.1 24.6 %collective-permute-start.12 = (bf16[256,3072]{1,0:T(8,128)(2,1)S(1)}, bf16[256,3072]{1,0:T(8,128)(2,1)S(1)}, u32[]{:S(2)}, u32[]{:S(2)}) collective-permute-start(bf16[256,3072]{1,0:T(8,128)(2,1)S(1)} %get-tuple-element.13), channel_id=1, source_target_pairs={{0,1},{1,0},{2,3},{3,2},{4,5},{5,4},{6,7},{7,6},{8,9},{9,8},{10,11... | collective-permute-start | bytes 4718600 | tf_op jit(solution)/shard_map/ppermute | solution.py:44
  100.5 10.9 %collective-permute-start.8 = (bf16[64,3072]{1,0:T(8,128)(2,1)S(1)}, bf16[64,3072]{1,0:T(8,128)(2,1)S(1)}, u32[]{:S(2)}, u32[]{:S(2)}) collective-permute-start(bf16[64,3072]{1,0:T(8,128)(2,1)S(1)} %fusion.4), channel_id=1, source_target_pairs={{0,2},{1,15},{2,0},{3,5},{4,6},{5,3},{6,4},{7,9},{8,10},{9,7},{10,... | collective-permute-start | bytes 1179656 | tf_op jit(solution)/shard_map/ppermute | solution.py:44
  101.8 14.1 %collective-permute-start.13 = (bf16[2,256,768]{2,1,0:T(8,128)(2,1)S(1)}, bf16[2,256,768]{2,1,0:T(8,128)(2,1)S(1)}, u32[]{:S(2)}, u32[]{:S(2)}) collective-permute-start(bf16[2,256,768]{2,1,0:T(8,128)(2,1)S(1)} %pad_maximum_fusion.2), channel_id=1, source_target_pairs={{0,1},{1,0},{2,3},{3,2},{4,5},{5,4},{6,7},{7,6},{8,9},{9,8},{10,11... | collective-permute-start | bytes 2359304 | tf_op jit(solution)/shard_map/ppermute | solution.py:44
  111.6 11.9 %collective-permute-start.9 = (bf16[64,3072]{1,0:T(8,128)(2,1)S(1)}, bf16[64,3072]{1,0:T(8,128)(2,1)S(1)}, u32[]{:S(2)}, u32[]{:S(2)}) collective-permute-start(bf16[64,3072]{1,0:T(8,128)(2,1)S(1)} %fusion.9), channel_id=1, source_target_pairs={{0,14},{1,3},{2,4},{3,1},{4,2},{5,7},{6,8},{7,5},{8,6},{9,11},{10,... | collective-permute-start | bytes 1179656 | tf_op jit(solution)/shard_map/ppermute | solution.py:44
  123.6 5.8 %collective-permute-start.10 = (bf16[32,3072]{1,0:T(8,128)(2,1)S(1)}, bf16[32,3072]{1,0:T(8,128)(2,1)S(1)}, u32[]{:S(2)}, u32[]{:S(2)}) collective-permute-start(bf16[32,3072]{1,0:T(8,128)(2,1)S(1)} %slice.181), channel_id=1, source_target_pairs={{0,2},{1,15},{2,0},{3,5},{4,6},{5,3},{6,4},{7,9},{8,10},{9,7},{10,... | collective-permute-start | bytes 589832 | tf_op jit(solution)/shard_map/ppermute | solution.py:44
  129.4 6.2 %collective-permute-start.11 = (bf16[16,3072]{1,0:T(8,128)(2,1)S(1)}, bf16[16,3072]{1,0:T(8,128)(2,1)S(1)}, u32[]{:S(2)}, u32[]{:S(2)}) collective-permute-start(bf16[16,3072]{1,0:T(8,128)(2,1)S(1)} %slice.182), channel_id=1, source_target_pairs={{0,16},{1,17},{2,18},{3,19},{4,20},{5,21},{6,22},{7,23},{8,24},{9,... | collective-permute-start | bytes 294920 | tf_op jit(solution)/shard_map/ppermute | solution.py:44

commit v2 on v1

--- a/solution.py
+++ b/solution.py
@@ -27,13 +27,14 @@
     swap_core = [(index(h, z, c), index(h, z, 1 - c)) for h, z, c in places]
     swap_half = [(index(h, z, c), index(1 - h, z, c)) for h, z, c in places]
 
-    def pairing(phase):
+    def pairing(phase, across):
         def partner(z, c):
             return z + 1 if (z + c + phase) % 2 == 0 else z - 1
 
-        return [(index(h, z, c), index(h, partner(z, c), c)) for h, z, c in places]
+        return [(index(h, z, c), index(h ^ across, partner(z, c), c)) for h, z, c in places]
 
-    return swap_core, swap_half, pairing(0), pairing(1)
+    pairs = [(pairing(phase, 0), pairing(phase, 1)) for phase in (0, 1)]
+    return swap_core, swap_half, *pairs
 
 
 def local(swap_core, swap_half, even, odd, rows, tokens, w_up, w_down, grad_out):
@@ -50,14 +51,20 @@
     grad_scale = 1.0 / math.sqrt(total_rows)
 
     mine = jnp.concatenate([tokens, grad_out], axis=1)
-    unit = jnp.concatenate([mine, swap(mine, swap_half)], axis=0)
-    first = jnp.concatenate([unit, swap(unit, even)], axis=0)
-    second = swap(first, odd)
-    third = swap(second, even)
-    fourth = swap(third, odd)
+    along = [mine, swap(mine, even[0])]
+    across = [swap(mine, swap_half), swap(mine, even[1])]
+    sent = jnp.concatenate(along, axis=0)
+    got = swap(sent, odd[0])
+    far = swap(sent, odd[1])
+    got, *across = lax.optimization_barrier((got, *across))
+    last = swap(got, even[0])
+    far2 = swap(got, even[1])
+    last, far = lax.optimization_barrier((last, far))
+    along += [got, last, swap(last, odd[0])]
+    across += [far, far2, swap(last, odd[1])]
     w_up_all = jnp.concatenate([w_up, swap(w_up, swap_core)], axis=1)
     w_down_all = jnp.concatenate([w_down, swap(w_down, swap_core)], axis=0)
-    both = jnp.concatenate([first, second, third, fourth], axis=0)
+    both = jnp.concatenate(along + across, axis=0)
     x_own, dy_own = both[:, :feats], both[:, feats:]
     units = both.shape[0] // rows
 
@@ -76,42 +83,45 @@
     hidden = spread[:, 0].reshape(rows * units, 2 * hid)
     grad_pre = spread[:, 1].reshape(rows * units, 2 * hid)
 
+    both, hidden, grad_pre = lax.optimization_barrier((both, hidden, grad_pre))
+    acts_other = swap(jnp.stack([hidden[:, hid:], grad_pre[:, hid:]]), swap_core)
+    both_other = swap(both, swap_core)
+    grad_up = jnp.zeros((), jnp.float32)
+    grad_down = jnp.zeros((), jnp.float32)
+    for tok, h, g in (
+        (both, hidden[:, :hid], grad_pre[:, :hid]),
+        (both_other, acts_other[0], acts_other[1]),
+    ):
+        grad_up += lax.dot_general(
+            tok[:, :feats], g, contract_first, preferred_element_type=jnp.float32
+        )
+        grad_down += lax.dot_general(
+            h, tok[:, feats:], contract_first, preferred_element_type=jnp.float32
+        )
+    grad_up = (grad_up * grad_scale).astype(jnp.bfloat16)
+    grad_down = (grad_down * grad_scale).astype(jnp.bfloat16)
+
     out_part = jnp.dot(hidden, w_down_all, preferred_element_type=jnp.float32)
     back_part = lax.dot_general(
         grad_pre, w_up_all, contract_last, preferred_element_type=jnp.float32
     )
     part = jnp.concatenate([out_part, back_part], axis=1)
-    held = first.shape[0]
-    blocks = [part[i * held : (i + 1) * held] for i in range(4)]
+    half = total_rows // 4
+    held = 2 * share
+    along = [part[i * held : (i + 1) * held] for i in range(4)]
+    across = [part[half + i * held : half + (i + 1) * held] for i in range(4)]
 
     def add(value, sent, perm):
         return value + swap(sent.astype(jnp.bfloat16), perm).astype(jnp.float32)
 
-    acc = add(blocks[2], blocks[3], odd)
-    acc = add(blocks[1], acc, even)
-    acc = add(blocks[0], acc, odd)
-    acc = add(acc[: held // 2], acc[held // 2 :], even)
-    acc = add(acc[:share], acc[share:], swap_half)
+    acc = add(add(along[2], across[3], odd[1]), along[3], odd[0])
+    acc, grad_down = lax.optimization_barrier((add(add(along[1], across[2], even[1]), acc, even[0]), grad_down))
+    acc, grad_up = lax.optimization_barrier((add(add(along[0], across[1], odd[1]), acc, odd[0]), grad_up))
+    own = add(acc[:share], across[0][:share], swap_half)
+    own = add(own, across[0][share:], even[1])
+    acc = add(own, acc[share:], even[0])
     output = acc[:, :feats].astype(jnp.bfloat16)
     grad_tokens = acc[:, feats:].astype(jnp.bfloat16)
-
-    both_other = swap(both, swap_core)
-    acts_other = swap(jnp.stack([hidden[:, hid:], grad_pre[:, hid:]]), swap_core)
-    both_all = jnp.concatenate([both, both_other], axis=0)
-    hidden_all = jnp.concatenate([hidden[:, :hid], acts_other[0]], axis=0)
-    grad_pre_all = jnp.concatenate([grad_pre[:, :hid], acts_other[1]], axis=0)
-    grad_up = (
-        lax.dot_general(
-            both_all[:, :feats], grad_pre_all, contract_first, preferred_element_type=jnp.float32
-        )
-        * grad_scale
-    ).astype(jnp.bfloat16)
-    grad_down = (
-        lax.dot_general(
-            hidden_all, both_all[:, feats:], contract_first, preferred_element_type=jnp.float32
-        )
-        * grad_scale
-    ).astype(jnp.bfloat16)
     return (output, grad_tokens, grad_up, grad_down)
 
 

time: 137 us -> 128 us (0.934)
  waiting for transfers between devices: 51.5 us -> 26.8 us
  starting transfers between devices: 28.7 us -> 41.7 us
  blocking collectives: 37.5 us -> 40.8 us
    ppermute x14 -> x22, waiting for transfers between devices: 51.5 us -> 26.8 us  [swap(): return lax.ppermute(value, 'col', perm)]
    ppermute x14 -> x22, starting transfers between devices: 28.7 us -> 41.7 us  [swap(): return lax.ppermute(value, 'col', perm)]
    all_to_all x1, blocking collectives: 17.8 us -> 19.8 us  [local(): lax.all_to_all(jnp.broadcast_to(pair[None], (rows,) + pair.shape), 'row',...]
    unnamed x11 -> x13, local copies, waits for them, and re-layouts: 3.88 us -> 2.9 us
    dot_general x2 -> x4, matrix products: 5.68 us -> 6.12 us  [the longest x2 3.08 us: local(): lax.dot_general(tok[:, :feats], g, contract_first, preferred_element_type...]
  transfers between devices with their start and end apart: 14 -> 22, of which waited for: 10 -> 8; matrix products, arithmetic and copies ran while one was open for 7% -> 8% of each run, Pallas kernels for 0% -> 0%
where the time goes in v2:
time: 128 us
  starting transfers between devices  41.7 us (33%)
  blocking collectives  40.8 us (32%)
  waiting for transfers between devices  26.8 us (21%)
  matrix products  11.7 us (9%)
  local copies, waits for them, and re-layouts  5.1 us (4%)
    ppermute x22, starting transfers between devices, swap(): return lax.ppermute(value, 'col', perm)  41.7 us
    ppermute x22, waiting for transfers between devices, swap(): return lax.ppermute(value, 'col', perm)  26.8 us
    all_to_all x1, blocking collectives, local(): parts = lax.all_to_all(parts, 'row', 0, 0)  21 us
    all_to_all x1, blocking collectives, local(): lax.all_to_all(jnp.broadcast_to(pair[None], (rows,) + pair.shape), 'row',...  19.8 us
    dot_general x2, matrix products, local(): lax.dot_general(tok[:, :feats], g, contract_first, preferred_element_type...  3.08 us
    dot_general x2, matrix products, local(): lax.dot_general(h, tok[:, feats:], contract_first, preferred_element_type...  3.04 us
    unnamed x13, local copies, waits for them, and re-layouts  2.9 us
  transfers between devices with their start and end apart: 22, of which 8 were waited for; matrix products, arithmetic and copies ran while one was open for 8% of the time, Pallas kernels for 0%

profile of v2, /device:TPU:8, one launch (start us, length us, event | category | flops | bytes accessed | tf_op | source)
XLA Modules:
  0.0 128.2 jit_solution(974808250967306573)
XLA Ops:
  0.6 0.8 constant_dynamic-update-slice_fusion.1
  1.4 0.8 constant_dynamic-update-slice_fusion
  2.2 4.5 %collective-permute-start.3 = (bf16[16,3072]{1,0:T(8,128)(2,1)S(1)}, bf16[16,3072]{1,0:T(8,128)(2,1)S(1)}, u32[]{:S(2)}, u32[]{:S(2)}) collective-permute-start(bf16[16,3072]{1,0:T(8,128)(2,1)S(1)} %get-tuple-element.40), channel_id=1, source_target_pairs={{0,18},{1,31},{2,16},{3,21},{4,22},{5,19},{6,20},{7,25},{8,26},{9,... | collective-permute-start | bytes 294920 | tf_op jit(solution)/shard_map/ppermute | solution.py:45
  6.7 0.5 collective-permute-start.2
  7.2 0.2 collective-permute-start
  7.4 3.2 %collective-permute-start.9 = (bf16[1536,768]{1,0:T(8,128)(2,1)}, bf16[1536,768]{1,0:T(8,128)(2,1)S(1)}, u32[]{:S(2)}, u32[]{:S(2)}) collective-permute-start(bf16[1536,768]{1,0:T(8,128)(2,1)} %param.5), channel_id=1, source_target_pairs={{0,1},{1,0},{2,3},{3,2},{4,5},{5,4},{6,7},{7,6},{8,9},{9,8},{10,11... | collective-permute-start | bytes 7077896 | tf_op jit(solution)/shard_map/ppermute | solution.py:45
  10.6 0.0 collective-permute-start.10
  10.6 1.8 %constant_dynamic-update-slice_fusion.14 = bf16[1536,1536]{1,0:T(8,128)(2,1)S(1)} fusion(bf16[1536,768]{1,0:T(8,128)(2,1)} %param.5), kind=kLoop, calls=%fused_computation.67 | loop fusion | bytes 4718592
  12.5 0.2 constant_dynamic-update-slice_fusion.16
  12.6 4.2 %collective-permute-start.1 = (bf16[32,3072]{1,0:T(8,128)(2,1)S(1)}, bf16[32,3072]{1,0:T(8,128)(2,1)S(1)}, u32[]{:S(2)}, u32[]{:S(2)}) collective-permute-start(bf16[32,3072]{1,0:T(8,128)(2,1)S(1)} %pad_maximum_fusion.3), channel_id=1, source_target_pairs={{0,14},{1,3},{2,4},{3,1},{4,2},{5,7},{6,8},{7,5},{8,6},{9,11},{10,... | collective-permute-start | bytes 589832 | tf_op jit(solution)/shard_map/ppermute | solution.py:45
  16.9 0.0 collective-permute-done.3
  16.9 2.6 %collective-permute-start.5 = (bf16[32,3072]{1,0:T(8,128)(2,1)S(1)}, bf16[32,3072]{1,0:T(8,128)(2,1)S(1)}, u32[]{:S(2)}, u32[]{:S(2)}) collective-permute-start(bf16[32,3072]{1,0:T(8,128)(2,1)S(1)} %pad_maximum_fusion.3), channel_id=1, source_target_pairs={{0,30},{1,19},{2,20},{3,17},{4,18},{5,23},{6,24},{7,21},{8,22},{9,... | collective-permute-start | bytes 589832 | tf_op jit(solution)/shard_map/ppermute | solution.py:45
  19.5 1.1 collective-permute-done.1
  20.5 1.3 %collective-permute-start.7 = (bf16[32,3072]{1,0:T(8,128)(2,1)S(1)}, bf16[32,3072]{1,0:T(8,128)(2,1)S(1)}, u32[]{:S(2)}, u32[]{:S(2)}) collective-permute-start(bf16[32,3072]{1,0:T(8,128)(2,1)S(1)} %collective-permute-done.1), channel_id=1, source_target_pairs={{0,18},{1,31},{2,16},{3,21},{4,22},{5,19},{6,20},{7,25},{8,26},{9,... | collective-permute-start | bytes 589832 | tf_op jit(solution)/shard_map/ppermute | solution.py:45
  21.9 3.1 %collective-permute-start.4 = (bf16[32,3072]{1,0:T(8,128)(2,1)S(1)}, bf16[32,3072]{1,0:T(8,128)(2,1)S(1)}, u32[]{:S(2)}, u32[]{:S(2)}) collective-permute-start(bf16[32,3072]{1,0:T(8,128)(2,1)S(1)} %collective-permute-done.1), channel_id=1, source_target_pairs={{0,2},{1,15},{2,0},{3,5},{4,6},{5,3},{6,4},{7,9},{8,10},{9,7},{10,... | collective-permute-start | bytes 589832 | tf_op jit(solution)/shard_map/ppermute | solution.py:45
  25.0 1.5 %collective-permute-done.5 = bf16[32,3072]{1,0:T(8,128)(2,1)S(1)} collective-permute-done((bf16[32,3072]{1,0:T(8,128)(2,1)S(1)}, bf16[32,3072]{1,0:T(8,128)(2,1)S(1)}, u32[]{:S(2)}, u32[]{:S(2)}) %collective-permute-start.5) | collective-permute-done | bytes 196640 | tf_op jit(solution)/shard_map/ppermute | solution.py:45
  26.6 5.4 %collective-permute-done.4 = bf16[32,3072]{1,0:T(8,128)(2,1)S(1)} collective-permute-done((bf16[32,3072]{1,0:T(8,128)(2,1)S(1)}, bf16[32,3072]{1,0:T(8,128)(2,1)S(1)}, u32[]{:S(2)}, u32[]{:S(2)}) %collective-permute-start.4) | collective-permute-done | bytes 196640 | tf_op jit(solution)/shard_map/ppermute | solution.py:45
  32.0 2.6 %collective-permute-start.8 = (bf16[32,3072]{1,0:T(8,128)(2,1)S(1)}, bf16[32,3072]{1,0:T(8,128)(2,1)S(1)}, u32[]{:S(2)}, u32[]{:S(2)}) collective-permute-start(bf16[32,3072]{1,0:T(8,128)(2,1)S(1)} %collective-permute-done.4), channel_id=1, source_target_pairs={{0,30},{1,19},{2,20},{3,17},{4,18},{5,23},{6,24},{7,21},{8,22},{9,... | collective-permute-start | bytes 589832 | tf_op jit(solution)/shard_map/ppermute | solution.py:45
  34.6 0.8 collective-permute-start.6
  35.4 6.1 %collective-permute-done.6 = bf16[32,3072]{1,0:T(8,128)(2,1)S(1)} collective-permute-done((bf16[32,3072]{1,0:T(8,128)(2,1)S(1)}, bf16[32,3072]{1,0:T(8,128)(2,1)S(1)}, u32[]{:S(2)}, u32[]{:S(2)}) %collective-permute-start.6) | collective-permute-done | bytes 196640 | tf_op jit(solution)/shard_map/ppermute | solution.py:45
  41.6 0.0 collective-permute-done.8
  41.6 0.0 collective-permute-done.9
  41.6 0.2 constant_dynamic-update-slice_fusion.13
  41.8 1.4 %convolution_convert_fusion.1 = bf16[256,1536]{1,0:T(8,128)(2,1)S(1)} fusion(bf16[1536,1536]{1,0:T(8,128)(2,1)S(1)} %constant_dynamic-update-slice_fusion.13, bf16[256,3072]{1,0:T(8,128)(2,1)S(1)} %constant_dynamic-update-slice_fusion.2), kind=kOutput, calls=%fused_computation.12 | convolution fusion | flops 1208352768 | bytes 6291456 | tf_op jit(solution)/shard_map/dot_general | solution.py:71
  43.2 0.2 constant_dynamic-update-slice_fusion.15
  43.4 1.4 %convolution_convert_fusion = bf16[256,1536]{1,0:T(8,128)(2,1)S(1)} fusion(bf16[1536,1536]{1,0:T(8,128)(2,1)S(1)} %constant_dynamic-update-slice_fusion.15, bf16[256,3072]{1,0:T(8,128)(2,1)S(1)} %constant_dynamic-update-slice_fusion.2), kind=kOutput, calls=%fused_computation.11 | convolution fusion | flops 1208352768 | bytes 6291456 | tf_op jit(solution)/shard_map/dot_general | solution.py:72
  44.8 0.2 pad_maximum_fusion.1
  45.0 21.0 %all_to_all.10 = bf16[8,2,32,1536]{3,2,1,0:T(8,128)(2,1)S(1)} all-to-all(bf16[8,2,32,1536]{3,2,1,0:T(8,128)(2,1)S(1)} %pad_maximum_fusion.1), channel_id=1, replica_groups=mesh['row'=8,'col'=32] {'row'}, dimensions={0} | all-to-all | bytes 3145728 | tf_op jit(solution)/shard_map/all_to_all | solution.py:78
  66.0 0.2 convert_reduce_fusion
  66.2 0.1 multiply_convert_fusion.2
  66.4 0.1 broadcast_in_dim.2
  66.5 19.8 %all_to_all.11 = bf16[8,2,32,1536]{3,2,1,0:T(8,128)(2,1)S(1)} all-to-all(bf16[8,2,32,1536]{3,2,1,0:T(8,128)(2,1)S(1)} %broadcast_in_dim.2), channel_id=1, replica_groups=mesh['row'=8,'col'=32] {'row'}, dimensions={0} | all-to-all | bytes 3145728 | tf_op jit(solution)/shard_map/all_to_all | solution.py:82
  86.4 0.1 fusion.30
  86.5 1.4 %fusion.33 = f32[256,1536]{1,0:T(8,128)S(1)} fusion(bf16[256,1536]{1,0:T(8,128)(2,1)S(1)} %bitcast.27, bf16[1536,1536]{1,0:T(8,128)(2,1)S(1)} %constant_dynamic-update-slice_fusion.13), kind=kOutput, calls=%fused_computation.75 | convolution fusion | flops 1207959552 | bytes 7077888 | tf_op jit(solution)/shard_map/dot_general | solution.py:105
  87.9 1.4 %fusion.32 = f32[256,1536]{1,0:T(8,128)S(1)} fusion(bf16[256,1536]{1,0:T(8,128)(2,1)S(1)} %bitcast.24, bf16[1536,1536]{1,0:T(8,128)(2,1)S(1)} %constant_dynamic-update-slice_fusion.15), kind=kOutput, calls=%fused_computation.74 | convolution fusion | flops 1207959552 | bytes 7077888 | tf_op jit(solution)/shard_map/dot_general | solution.py:104
  89.3 0.1 slice_bitcast_fusion.4
  89.4 0.2 fusion
  89.6 0.1 fusion.29
  89.6 0.1 pad_maximum_fusion.2
  89.7 0.1 collective-permute-start.16
  89.8 0.1 collective-permute-start.14
  89.9 5.4 %collective-permute-start.13 = (bf16[32,3072]{1,0:T(8,128)(2,1)S(1)}, bf16[32,3072]{1,0:T(8,128)(2,1)S(1)}, u32[]{:S(2)}, u32[]{:S(2)}) collective-permute-start(bf16[32,3072]{1,0:T(8,128)(2,1)S(1)} %get-tuple-element.32), channel_id=1, source_target_pairs={{0,30},{1,19},{2,20},{3,17},{4,18},{5,23},{6,24},{7,21},{8,22},{9,... | collective-permute-start | bytes 589832 | tf_op jit(solution)/shard_map/ppermute | solution.py:45
  95.3 1.4 %collective-permute-start.12 = (bf16[32,3072]{1,0:T(8,128)(2,1)S(1)}, bf16[32,3072]{1,0:T(8,128)(2,1)S(1)}, u32[]{:S(2)}, u32[]{:S(2)}) collective-permute-start(bf16[32,3072]{1,0:T(8,128)(2,1)S(1)} %get-tuple-element.33), channel_id=1, source_target_pairs={{0,18},{1,31},{2,16},{3,21},{4,22},{5,19},{6,20},{7,25},{8,26},{9,... | collective-permute-start | bytes 589832 | tf_op jit(solution)/shard_map/ppermute | solution.py:45
  96.7 0.0 collective-permute-start.17
  96.8 0.8 fusion.7
  97.6 0.0 collective-permute-done.14
  97.6 4.7 %collective-permute-done.13 = bf16[32,3072]{1,0:T(8,128)(2,1)S(1)} collective-permute-done((bf16[32,3072]{1,0:T(8,128)(2,1)S(1)}, bf16[32,3072]{1,0:T(8,128)(2,1)S(1)}, u32[]{:S(2)}, u32[]{:S(2)}) %collective-permute-start.13) | collective-permute-done | bytes 196640 | tf_op jit(solution)/shard_map/ppermute | solution.py:45
  102.3 0.1 fusion.18
  102.3 4.1 %collective-permute-start.15 = (bf16[32,3072]{1,0:T(8,128)(2,1)S(1)}, bf16[32,3072]{1,0:T(8,128)(2,1)S(1)}, u32[]{:S(2)}, u32[]{:S(2)}) collective-permute-start(bf16[32,3072]{1,0:T(8,128)(2,1)S(1)} %fusion.18), channel_id=1, source_target_pairs={{0,2},{1,15},{2,0},{3,5},{4,6},{5,3},{6,4},{7,9},{8,10},{9,7},{10,... | collective-permute-start | bytes 589832 | tf_op jit(solution)/shard_map/ppermute | solution.py:45
  106.4 0.8 fusion.5
  107.2 1.3 %collective-permute-start.19 = (bf16[16,3072]{1,0:T(8,128)(2,1)S(1)}, bf16[16,3072]{1,0:T(8,128)(2,1)S(1)}, u32[]{:S(2)}, u32[]{:S(2)}) collective-permute-start(bf16[16,3072]{1,0:T(8,128)(2,1)S(1)} %get-tuple-element.28), channel_id=1, source_target_pairs={{0,16},{1,17},{2,18},{3,19},{4,20},{5,21},{6,22},{7,23},{8,24},{9,... | collective-permute-start | bytes 294920 | tf_op jit(solution)/shard_map/ppermute | solution.py:45
  108.6 0.0 collective-permute-done.12
  108.6 1.7 %collective-permute-start.20 = (bf16[16,3072]{1,0:T(8,128)(2,1)S(1)}, bf16[16,3072]{1,0:T(8,128)(2,1)S(1)}, u32[]{:S(2)}, u32[]{:S(2)}) collective-permute-start(bf16[16,3072]{1,0:T(8,128)(2,1)S(1)} %get-tuple-element.29), channel_id=1, source_target_pairs={{0,18},{1,31},{2,16},{3,21},{4,22},{5,19},{6,20},{7,25},{8,26},{9,... | collective-permute-start | bytes 294920 | tf_op jit(solution)/shard_map/ppermute | solution.py:45
  110.3 3.2 %collective-permute-start.11 = (bf16[32,3072]{1,0:T(8,128)(2,1)S(1)}, bf16[32,3072]{1,0:T(8,128)(2,1)S(1)}, u32[]{:S(2)}, u32[]{:S(2)}) collective-permute-start(bf16[32,3072]{1,0:T(8,128)(2,1)S(1)} %get-tuple-element.30), channel_id=1, source_target_pairs={{0,30},{1,19},{2,20},{3,17},{4,18},{5,23},{6,24},{7,21},{8,22},{9,... | collective-permute-start | bytes 589832 | tf_op jit(solution)/shard_map/ppermute | solution.py:45
  113.5 0.1 fusion.14
  113.6 2.2 %multiply_convert_fusion.1 = bf16[768,1536]{1,0:T(8,128)(2,1)} fusion(f32[768,1536]{1,0:T(8,128)S(1)} %fusion.7, bf16[256,3072]{1,0:T(8,128)(2,1)S(1)} %collective-permute-done.17, bf16[2,256,768]{2,1,0:T(8,128)(2,1)S(1)} %collective-permute-done.16), kind=kOutput, calls=%fused_computation.8 | convolution fusion | flops 607518720 | bytes 8257536 | tf_op jit(solution)/shard_map/dot_general | solution.py:98
  115.8 0.7 collective-permute-start.18
  116.6 2.2 %multiply_convert_fusion = bf16[1536,768]{1,0:T(8,128)(2,1)} fusion(f32[1536,768]{1,0:T(8,128)S(1)} %fusion.5, bf16[256,3072]{1,0:T(8,128)(2,1)S(1)} %collective-permute-done.17, bf16[2,256,768]{2,1,0:T(8,128)(2,1)S(1)} %collective-permute-done.16), kind=kOutput, calls=%fused_computation.7 | convolution fusion | flops 607518720 | bytes 8257536 | tf_op jit(solution)/shard_map/dot_general | solution.py:95
  118.8 1.0 collective-permute-done.11
  119.8 2.9 %collective-permute-done.18 = bf16[32,3072]{1,0:T(8,128)(2,1)S(1)} collective-permute-done((bf16[32,3072]{1,0:T(8,128)(2,1)S(1)}, bf16[32,3072]{1,0:T(8,128)(2,1)S(1)}, u32[]{:S(2)}, u32[]{:S(2)}) %collective-permute-start.18) | collective-permute-done | bytes 196640 | tf_op jit(solution)/shard_map/ppermute | solution.py:45
  122.7 0.1 fusion.11
  122.8 0.6 collective-permute-start.21
  123.4 4.1 %collective-permute-done.21 = bf16[16,3072]{1,0:T(8,128)(2,1)S(1)} collective-permute-done((bf16[16,3072]{1,0:T(8,128)(2,1)S(1)}, bf16[16,3072]{1,0:T(8,128)(2,1)S(1)}, u32[]{:S(2)}, u32[]{:S(2)}) %collective-permute-start.21) | collective-permute-done | bytes 98336 | tf_op jit(solution)/shard_map/ppermute | solution.py:45
  127.6 0.6 fusion.31
  (25 shorter events, 0.3 us)
Async XLA Ops:
  2.2 10.2 %copy-start = (bf16[768,1536]{1,0:T(8,128)(2,1)S(1)}, bf16[768,1536]{1,0:T(8,128)(2,1)}, u32[]{:S(2)}) copy-start(bf16[768,1536]{1,0:T(8,128)(2,1)} %param.6) | copy-start | bytes 7077892
  2.2 14.7 %collective-permute-start.3 = (bf16[16,3072]{1,0:T(8,128)(2,1)S(1)}, bf16[16,3072]{1,0:T(8,128)(2,1)S(1)}, u32[]{:S(2)}, u32[]{:S(2)}) collective-permute-start(bf16[16,3072]{1,0:T(8,128)(2,1)S(1)} %get-tuple-element.40), channel_id=1, source_target_pairs={{0,18},{1,31},{2,16},{3,21},{4,22},{5,19},{6,20},{7,25},{8,26},{9,... | collective-permute-start | bytes 294920 | tf_op jit(solution)/shard_map/ppermute | solution.py:45
  6.7 12.8 %collective-permute-start.2 = (bf16[16,3072]{1,0:T(8,128)(2,1)S(1)}, bf16[16,3072]{1,0:T(8,128)(2,1)S(1)}, u32[]{:S(2)}, u32[]{:S(2)}) collective-permute-start(bf16[16,3072]{1,0:T(8,128)(2,1)S(1)} %get-tuple-element.40), channel_id=1, source_target_pairs={{0,16},{1,17},{2,18},{3,19},{4,20},{5,21},{6,22},{7,23},{8,24},{9,... | collective-permute-start | bytes 294920 | tf_op jit(solution)/shard_map/ppermute | solution.py:45
  7.2 5.4 %collective-permute-start = (bf16[16,3072]{1,0:T(8,128)(2,1)S(1)}, bf16[16,3072]{1,0:T(8,128)(2,1)S(1)}, u32[]{:S(2)}, u32[]{:S(2)}) collective-permute-start(bf16[16,3072]{1,0:T(8,128)(2,1)S(1)} %get-tuple-element.40), channel_id=1, source_target_pairs={{0,2},{1,15},{2,0},{3,5},{4,6},{5,3},{6,4},{7,9},{8,10},{9,7},{10,... | collective-permute-start | bytes 294920 | tf_op jit(solution)/shard_map/ppermute | solution.py:45
  7.4 34.2 %collective-permute-start.9 = (bf16[1536,768]{1,0:T(8,128)(2,1)}, bf16[1536,768]{1,0:T(8,128)(2,1)S(1)}, u32[]{:S(2)}, u32[]{:S(2)}) collective-permute-start(bf16[1536,768]{1,0:T(8,128)(2,1)} %param.5), channel_id=1, source_target_pairs={{0,1},{1,0},{2,3},{3,2},{4,5},{5,4},{6,7},{7,6},{8,9},{9,8},{10,11... | collective-permute-start | bytes 7077896 | tf_op jit(solution)/shard_map/ppermute | solution.py:45
  10.6 32.6 %collective-permute-start.10 = (bf16[768,1536]{1,0:T(8,128)(2,1)}, bf16[768,1536]{1,0:T(8,128)(2,1)S(1)}, u32[]{:S(2)}, u32[]{:S(2)}) collective-permute-start(bf16[768,1536]{1,0:T(8,128)(2,1)} %param.6), channel_id=1, source_target_pairs={{0,1},{1,0},{2,3},{3,2},{4,5},{5,4},{6,7},{7,6},{8,9},{9,8},{10,11... | collective-permute-start | bytes 7077896 | tf_op jit(solution)/shard_map/ppermute | solution.py:45
  12.6 7.9 %collective-permute-start.1 = (bf16[32,3072]{1,0:T(8,128)(2,1)S(1)}, bf16[32,3072]{1,0:T(8,128)(2,1)S(1)}, u32[]{:S(2)}, u32[]{:S(2)}) collective-permute-start(bf16[32,3072]{1,0:T(8,128)(2,1)S(1)} %pad_maximum_fusion.3), channel_id=1, source_target_pairs={{0,14},{1,3},{2,4},{3,1},{4,2},{5,7},{6,8},{7,5},{8,6},{9,11},{10,... | collective-permute-start | bytes 589832 | tf_op jit(solution)/shard_map/ppermute | solution.py:45
  16.9 9.7 %collective-permute-start.5 = (bf16[32,3072]{1,0:T(8,128)(2,1)S(1)}, bf16[32,3072]{1,0:T(8,128)(2,1)S(1)}, u32[]{:S(2)}, u32[]{:S(2)}) collective-permute-start(bf16[32,3072]{1,0:T(8,128)(2,1)S(1)} %pad_maximum_fusion.3), channel_id=1, source_target_pairs={{0,30},{1,19},{2,20},{3,17},{4,18},{5,23},{6,24},{7,21},{8,22},{9,... | collective-permute-start | bytes 589832 | tf_op jit(solution)/shard_map/ppermute | solution.py:45
  20.5 21.0 %collective-permute-start.7 = (bf16[32,3072]{1,0:T(8,128)(2,1)S(1)}, bf16[32,3072]{1,0:T(8,128)(2,1)S(1)}, u32[]{:S(2)}, u32[]{:S(2)}) collective-permute-start(bf16[32,3072]{1,0:T(8,128)(2,1)S(1)} %collective-permute-done.1), channel_id=1, source_target_pairs={{0,18},{1,31},{2,16},{3,21},{4,22},{5,19},{6,20},{7,25},{8,26},{9,... | collective-permute-start | bytes 589832 | tf_op jit(solution)/shard_map/ppermute | solution.py:45
  21.9 10.1 %collective-permute-start.4 = (bf16[32,3072]{1,0:T(8,128)(2,1)S(1)}, bf16[32,3072]{1,0:T(8,128)(2,1)S(1)}, u32[]{:S(2)}, u32[]{:S(2)}) collective-permute-start(bf16[32,3072]{1,0:T(8,128)(2,1)S(1)} %collective-permute-done.1), channel_id=1, source_target_pairs={{0,2},{1,15},{2,0},{3,5},{4,6},{5,3},{6,4},{7,9},{8,10},{9,7},{10,... | collective-permute-start | bytes 589832 | tf_op jit(solution)/shard_map/ppermute | solution.py:45
  32.0 9.6 %collective-permute-start.8 = (bf16[32,3072]{1,0:T(8,128)(2,1)S(1)}, bf16[32,3072]{1,0:T(8,128)(2,1)S(1)}, u32[]{:S(2)}, u32[]{:S(2)}) collective-permute-start(bf16[32,3072]{1,0:T(8,128)(2,1)S(1)} %collective-permute-done.4), channel_id=1, source_target_pairs={{0,30},{1,19},{2,20},{3,17},{4,18},{5,23},{6,24},{7,21},{8,22},{9,... | collective-permute-start | bytes 589832 | tf_op jit(solution)/shard_map/ppermute | solution.py:45
  34.6 6.9 %collective-permute-start.6 = (bf16[32,3072]{1,0:T(8,128)(2,1)S(1)}, bf16[32,3072]{1,0:T(8,128)(2,1)S(1)}, u32[]{:S(2)}, u32[]{:S(2)}) collective-permute-start(bf16[32,3072]{1,0:T(8,128)(2,1)S(1)} %collective-permute-done.4), channel_id=1, source_target_pairs={{0,14},{1,3},{2,4},{3,1},{4,2},{5,7},{6,8},{7,5},{8,6},{9,11},{10,... | collective-permute-start | bytes 589832 | tf_op jit(solution)/shard_map/ppermute | solution.py:45
  89.7 23.9 %collective-permute-start.16 = (bf16[2,256,768]{2,1,0:T(8,128)(2,1)S(1)}, bf16[2,256,768]{2,1,0:T(8,128)(2,1)S(1)}, u32[]{:S(2)}, u32[]{:S(2)}) collective-permute-start(bf16[2,256,768]{2,1,0:T(8,128)(2,1)S(1)} %pad_maximum_fusion.2), channel_id=1, source_target_pairs={{0,1},{1,0},{2,3},{3,2},{4,5},{5,4},{6,7},{7,6},{8,9},{9,8},{10,11... | collective-permute-start | bytes 2359304 | tf_op jit(solution)/shard_map/ppermute | solution.py:45
  89.8 7.7 %collective-permute-start.14 = (bf16[32,3072]{1,0:T(8,128)(2,1)S(1)}, bf16[32,3072]{1,0:T(8,128)(2,1)S(1)}, u32[]{:S(2)}, u32[]{:S(2)}) collective-permute-start(bf16[32,3072]{1,0:T(8,128)(2,1)S(1)} %get-tuple-element.31), channel_id=1, source_target_pairs={{0,14},{1,3},{2,4},{3,1},{4,2},{5,7},{6,8},{7,5},{8,6},{9,11},{10,... | collective-permute-start | bytes 589832 | tf_op jit(solution)/shard_map/ppermute | solution.py:45
  89.9 12.3 %collective-permute-start.13 = (bf16[32,3072]{1,0:T(8,128)(2,1)S(1)}, bf16[32,3072]{1,0:T(8,128)(2,1)S(1)}, u32[]{:S(2)}, u32[]{:S(2)}) collective-permute-start(bf16[32,3072]{1,0:T(8,128)(2,1)S(1)} %get-tuple-element.32), channel_id=1, source_target_pairs={{0,30},{1,19},{2,20},{3,17},{4,18},{5,23},{6,24},{7,21},{8,22},{9,... | collective-permute-start | bytes 589832 | tf_op jit(solution)/shard_map/ppermute | solution.py:45
  95.3 13.2 %collective-permute-start.12 = (bf16[32,3072]{1,0:T(8,128)(2,1)S(1)}, bf16[32,3072]{1,0:T(8,128)(2,1)S(1)}, u32[]{:S(2)}, u32[]{:S(2)}) collective-permute-start(bf16[32,3072]{1,0:T(8,128)(2,1)S(1)} %get-tuple-element.33), channel_id=1, source_target_pairs={{0,18},{1,31},{2,16},{3,21},{4,22},{5,19},{6,20},{7,25},{8,26},{9,... | collective-permute-start | bytes 589832 | tf_op jit(solution)/shard_map/ppermute | solution.py:45
  96.7 16.9 %collective-permute-start.17 = (bf16[256,3072]{1,0:T(8,128)(2,1)S(1)}, bf16[256,3072]{1,0:T(8,128)(2,1)S(1)}, u32[]{:S(2)}, u32[]{:S(2)}) collective-permute-start(bf16[256,3072]{1,0:T(8,128)(2,1)S(1)} %constant_dynamic-update-slice_fusion.2), channel_id=1, source_target_pairs={{0,1},{1,0},{2,3},{3,2},{4,5},{5,4},{6,7},{7,6},{8,9},{9,8},{10,11... | collective-permute-start | bytes 4718600 | tf_op jit(solution)/shard_map/ppermute | solution.py:45
  102.3 8.0 %collective-permute-start.15 = (bf16[32,3072]{1,0:T(8,128)(2,1)S(1)}, bf16[32,3072]{1,0:T(8,128)(2,1)S(1)}, u32[]{:S(2)}, u32[]{:S(2)}) collective-permute-start(bf16[32,3072]{1,0:T(8,128)(2,1)S(1)} %fusion.18), channel_id=1, source_target_pairs={{0,2},{1,15},{2,0},{3,5},{4,6},{5,3},{6,4},{7,9},{8,10},{9,7},{10,... | collective-permute-start | bytes 589832 | tf_op jit(solution)/shard_map/ppermute | solution.py:45
  107.2 16.2 %collective-permute-start.19 = (bf16[16,3072]{1,0:T(8,128)(2,1)S(1)}, bf16[16,3072]{1,0:T(8,128)(2,1)S(1)}, u32[]{:S(2)}, u32[]{:S(2)}) collective-permute-start(bf16[16,3072]{1,0:T(8,128)(2,1)S(1)} %get-tuple-element.28), channel_id=1, source_target_pairs={{0,16},{1,17},{2,18},{3,19},{4,20},{5,21},{6,22},{7,23},{8,24},{9,... | collective-permute-start | bytes 294920 | tf_op jit(solution)/shard_map/ppermute | solution.py:45
  108.6 14.8 %collective-permute-start.20 = (bf16[16,3072]{1,0:T(8,128)(2,1)S(1)}, bf16[16,3072]{1,0:T(8,128)(2,1)S(1)}, u32[]{:S(2)}, u32[]{:S(2)}) collective-permute-start(bf16[16,3072]{1,0:T(8,128)(2,1)S(1)} %get-tuple-element.29), channel_id=1, source_target_pairs={{0,18},{1,31},{2,16},{3,21},{4,22},{5,19},{6,20},{7,25},{8,26},{9,... | collective-permute-start | bytes 294920 | tf_op jit(solution)/shard_map/ppermute | solution.py:45
  110.3 9.5 %collective-permute-start.11 = (bf16[32,3072]{1,0:T(8,128)(2,1)S(1)}, bf16[32,3072]{1,0:T(8,128)(2,1)S(1)}, u32[]{:S(2)}, u32[]{:S(2)}) collective-permute-start(bf16[32,3072]{1,0:T(8,128)(2,1)S(1)} %get-tuple-element.30), channel_id=1, source_target_pairs={{0,30},{1,19},{2,20},{3,17},{4,18},{5,23},{6,24},{7,21},{8,22},{9,... | collective-permute-start | bytes 589832 | tf_op jit(solution)/shard_map/ppermute | solution.py:45
  115.8 6.9 %collective-permute-start.18 = (bf16[32,3072]{1,0:T(8,128)(2,1)S(1)}, bf16[32,3072]{1,0:T(8,128)(2,1)S(1)}, u32[]{:S(2)}, u32[]{:S(2)}) collective-permute-start(bf16[32,3072]{1,0:T(8,128)(2,1)S(1)} %fusion.14), channel_id=1, source_target_pairs={{0,14},{1,3},{2,4},{3,1},{4,2},{5,7},{6,8},{7,5},{8,6},{9,11},{10,... | collective-permute-start | bytes 589832 | tf_op jit(solution)/shard_map/ppermute | solution.py:45
  122.8 4.7 %collective-permute-start.21 = (bf16[16,3072]{1,0:T(8,128)(2,1)S(1)}, bf16[16,3072]{1,0:T(8,128)(2,1)S(1)}, u32[]{:S(2)}, u32[]{:S(2)}) collective-permute-start(bf16[16,3072]{1,0:T(8,128)(2,1)S(1)} %slice.217), channel_id=1, source_target_pairs={{0,2},{1,15},{2,0},{3,5},{4,6},{5,3},{6,4},{7,9},{8,10},{9,7},{10,... | collective-permute-start | bytes 294920 | tf_op jit(solution)/shard_map/ppermute | solution.py:45

commit v3 on v2

--- a/solution.py
+++ b/solution.py
@@ -50,21 +50,26 @@
     hid = w_up.shape[1]
     grad_scale = 1.0 / math.sqrt(total_rows)
 
+    def after(value, *others):
+        return lax.optimization_barrier((value, *others))[0]
+
     mine = jnp.concatenate([tokens, grad_out], axis=1)
-    along = [mine, swap(mine, even[0])]
-    across = [swap(mine, swap_half), swap(mine, even[1])]
-    sent = jnp.concatenate(along, axis=0)
-    got = swap(sent, odd[0])
-    far = swap(sent, odd[1])
-    got, *across = lax.optimization_barrier((got, *across))
-    last = swap(got, even[0])
-    far2 = swap(got, even[1])
-    last, far = lax.optimization_barrier((last, far))
-    along += [got, last, swap(last, odd[0])]
-    across += [far, far2, swap(last, odd[1])]
+    near1 = swap(mine, even[0])
+    far0 = swap(mine, swap_half)
+    far1 = swap(mine, even[1])
+    near01 = jnp.concatenate([mine, near1], axis=0)
+    near2 = swap(near01, odd[0])
+    far2 = swap(near01, odd[1])
+    near2, far0, far1 = lax.optimization_barrier((near2, far0, far1))
+    near3 = swap(near2, even[0])
+    far3 = swap(near2, even[1])
+    near3, far2 = lax.optimization_barrier((near3, far2))
+    near4 = swap(near3, odd[0])
+    far4 = swap(near3, odd[1])
+    w_up, w_down = lax.optimization_barrier((w_up, w_down, near2))[:2]
     w_up_all = jnp.concatenate([w_up, swap(w_up, swap_core)], axis=1)
     w_down_all = jnp.concatenate([w_down, swap(w_down, swap_core)], axis=0)
-    both = jnp.concatenate(along + across, axis=0)
+    both = jnp.concatenate([near01, far0, far1, near2, far2, near3, far3, near4, far4], axis=0)
     x_own, dy_own = both[:, :feats], both[:, feats:]
     units = both.shape[0] // rows
 
@@ -84,10 +89,32 @@
     grad_pre = spread[:, 1].reshape(rows * units, 2 * hid)
 
     both, hidden, grad_pre = lax.optimization_barrier((both, hidden, grad_pre))
-    acts_other = swap(jnp.stack([hidden[:, hid:], grad_pre[:, hid:]]), swap_core)
-    both_other = swap(both, swap_core)
-    grad_up = jnp.zeros((), jnp.float32)
-    grad_down = jnp.zeros((), jnp.float32)
+
+    out_part = jnp.dot(hidden, w_down_all, preferred_element_type=jnp.float32)
+    back_part = lax.dot_general(
+        grad_pre, w_up_all, contract_last, preferred_element_type=jnp.float32
+    )
+    part = jnp.concatenate([out_part, back_part], axis=1)
+    held = 2 * share
+
+    def rows_of(i, j):
+        return jnp.concatenate([part[k * share : (k + 1) * share] for k in (i, j)], axis=0)
+
+
+    def moved(sent, perm, *others):
+        return swap(after(sent.astype(jnp.bfloat16), *others), perm)
+
+    near01, far01 = rows_of(0, 4), rows_of(2, 6)
+    near2, far2 = rows_of(1, 8), rows_of(3, 10)
+    near3, far3 = rows_of(5, 12), rows_of(7, 14)
+    near4, far4 = rows_of(9, 13), rows_of(11, 15)
+    far4 = moved(far4, even[1])
+    near3 = near3 + far4 + moved(near4, even[0])
+
+    acts_sent = jnp.stack([hidden[:, hid:], grad_pre[:, hid:]])
+    acts_other = swap(after(acts_sent, near3), swap_core)
+    both_other = swap(after(both, near3), swap_core)
+    grad_up = grad_down = 0.0
     for tok, h, g in (
         (both, hidden[:, :hid], grad_pre[:, :hid]),
         (both_other, acts_other[0], acts_other[1]),
@@ -101,25 +128,17 @@
     grad_up = (grad_up * grad_scale).astype(jnp.bfloat16)
     grad_down = (grad_down * grad_scale).astype(jnp.bfloat16)
 
-    out_part = jnp.dot(hidden, w_down_all, preferred_element_type=jnp.float32)
-    back_part = lax.dot_general(
-        grad_pre, w_up_all, contract_last, preferred_element_type=jnp.float32
-    )
-    part = jnp.concatenate([out_part, back_part], axis=1)
-    half = total_rows // 4
-    held = 2 * share
-    along = [part[i * held : (i + 1) * held] for i in range(4)]
-    across = [part[half + i * held : half + (i + 1) * held] for i in range(4)]
-
-    def add(value, sent, perm):
-        return value + swap(sent.astype(jnp.bfloat16), perm).astype(jnp.float32)
-
-    acc = add(add(along[2], across[3], odd[1]), along[3], odd[0])
-    acc, grad_down = lax.optimization_barrier((add(add(along[1], across[2], even[1]), acc, even[0]), grad_down))
-    acc, grad_up = lax.optimization_barrier((add(add(along[0], across[1], odd[1]), acc, odd[0]), grad_up))
-    own = add(acc[:share], across[0][:share], swap_half)
-    own = add(own, across[0][share:], even[1])
-    acc = add(own, acc[share:], even[0])
+    far3 = moved(far3, odd[1], far4)
+    near2 = near2 + far3 + moved(near3, odd[0])
+    far2 = moved(far2, even[1], far3)
+    far0 = moved(far01[:share], swap_half, far4)
+    far1 = moved(far01[share:], odd[1], far3)
+    near01 = near01 + far2 + moved(near2, even[0])
+    acc = near01[:share] + far0 + far1
+    near1 = moved(near01[share:], odd[0])
+    near1, grad_down = lax.optimization_barrier((near1, grad_down))
+    near1, grad_up = lax.optimization_barrier((near1, grad_up))
+    acc = acc + near1
     output = acc[:, :feats].astype(jnp.bfloat16)
     grad_tokens = acc[:, feats:].astype(jnp.bfloat16)
     return (output, grad_tokens, grad_up, grad_down)

time: 128 us -> 127 us (level)
  blocking collectives: 40.8 us -> 38.4 us
  starting transfers between devices: 41.7 us -> 39.4 us
  waiting for transfers between devices: 26.8 us -> 29.1 us
    ppermute x22, starting transfers between devices: 41.7 us -> 39.4 us  [swap(): return lax.ppermute(value, 'col', perm)]
    ppermute x22, waiting for transfers between devices: 26.8 us -> 29.1 us  [swap(): return lax.ppermute(value, 'col', perm)]
    all_to_all x1, blocking collectives: 19.8 us -> 18.4 us  [local(): lax.all_to_all(jnp.broadcast_to(pair[None], (rows,) + pair.shape), 'row',...]
  transfers between devices with their start and end apart: 22 -> 22, of which waited for: 8 -> 7; matrix products, arithmetic and copies ran while one was open for 8% -> 8% of each run, Pallas kernels for 0% -> 0%
where the time goes in v3:
time: 127 us; the launch traced here: 126 us
  starting transfers between devices  39.4 us (31%)
  blocking collectives  38.4 us (30%)
  waiting for transfers between devices  29.1 us (23%)
  matrix products  11.7 us (9%)
  local copies, waits for them, and re-layouts  5.1 us (4%)
    ppermute x22, starting transfers between devices, swap(): return lax.ppermute(value, 'col', perm)  39.4 us
    ppermute x22, waiting for transfers between devices, swap(): return lax.ppermute(value, 'col', perm)  29.1 us
    all_to_all x1, blocking collectives, local(): parts = lax.all_to_all(parts, 'row', 0, 0)  20.1 us
    all_to_all x1, blocking collectives, local(): lax.all_to_all(jnp.broadcast_to(pair[None], (rows,) + pair.shape), 'row',...  18.4 us
    dot_general x2, matrix products, local(): lax.dot_general(tok[:, :feats], g, contract_first, preferred_element_type...  3.08 us
    dot_general x2, matrix products, local(): lax.dot_general(h, tok[:, feats:], contract_first, preferred_element_type...  3.03 us
    unnamed x13, local copies, waits for them, and re-layouts  2.9 us
  transfers between devices with their start and end apart: 22, of which 7 were waited for; matrix products, arithmetic and copies ran while one was open for 8% of the time, Pallas kernels for 0%

profile of v3, /device:TPU:8, one launch (start us, length us, event | category | flops | bytes accessed | tf_op | source)
XLA Modules:
  0.0 125.9 jit_solution(8422286010638967564)
XLA Ops:
  0.6 0.8 constant_dynamic-update-slice_fusion.1
  1.4 0.8 constant_dynamic-update-slice_fusion
  2.2 1.9 %collective-permute-start = (bf16[16,3072]{1,0:T(8,128)(2,1)S(1)}, bf16[16,3072]{1,0:T(8,128)(2,1)S(1)}, u32[]{:S(2)}, u32[]{:S(2)}) collective-permute-start(bf16[16,3072]{1,0:T(8,128)(2,1)S(1)} %get-tuple-element.66), channel_id=1, source_target_pairs={{0,2},{1,15},{2,0},{3,5},{4,6},{5,3},{6,4},{7,9},{8,10},{9,7},{10,... | collective-permute-start | bytes 294920 | tf_op jit(solution)/shard_map/ppermute | solution.py:45
  4.2 2.6 %collective-permute-start.3 = (bf16[16,3072]{1,0:T(8,128)(2,1)S(1)}, bf16[16,3072]{1,0:T(8,128)(2,1)S(1)}, u32[]{:S(2)}, u32[]{:S(2)}) collective-permute-start(bf16[16,3072]{1,0:T(8,128)(2,1)S(1)} %get-tuple-element.66), channel_id=1, source_target_pairs={{0,18},{1,31},{2,16},{3,21},{4,22},{5,19},{6,20},{7,25},{8,26},{9,... | collective-permute-start | bytes 294920 | tf_op jit(solution)/shard_map/ppermute | solution.py:45
  6.7 0.5 collective-permute-start.2
  7.2 0.0 collective-permute-done
  7.3 8.4 %collective-permute-start.5 = (bf16[32,3072]{1,0:T(8,128)(2,1)S(1)}, bf16[32,3072]{1,0:T(8,128)(2,1)S(1)}, u32[]{:S(2)}, u32[]{:S(2)}) collective-permute-start(bf16[32,3072]{1,0:T(8,128)(2,1)S(1)} %pad_maximum_fusion.3), channel_id=1, source_target_pairs={{0,30},{1,19},{2,20},{3,17},{4,18},{5,23},{6,24},{7,21},{8,22},{9,... | collective-permute-start | bytes 589832 | tf_op jit(solution)/shard_map/ppermute | solution.py:45
  15.7 0.0 copy-start
  15.7 0.0 collective-permute-done.3
  15.7 0.0 collective-permute-done.2
  15.7 6.8 %collective-permute-done.1 = bf16[32,3072]{1,0:T(8,128)(2,1)S(1)} collective-permute-done((bf16[32,3072]{1,0:T(8,128)(2,1)S(1)}, bf16[32,3072]{1,0:T(8,128)(2,1)S(1)}, u32[]{:S(2)}, u32[]{:S(2)}) %collective-permute-start.1) | collective-permute-done | bytes 196640 | tf_op jit(solution)/shard_map/ppermute | solution.py:45
  22.5 0.0 collective-permute-start.6
  22.5 2.0 %collective-permute-start.4 = (bf16[32,3072]{1,0:T(8,128)(2,1)S(1)}, bf16[32,3072]{1,0:T(8,128)(2,1)S(1)}, u32[]{:S(2)}, u32[]{:S(2)}) collective-permute-start(bf16[32,3072]{1,0:T(8,128)(2,1)S(1)} %collective-permute-done.1), channel_id=1, source_target_pairs={{0,2},{1,15},{2,0},{3,5},{4,6},{5,3},{6,4},{7,9},{8,10},{9,7},{10,... | collective-permute-start | bytes 589832 | tf_op jit(solution)/shard_map/ppermute | solution.py:45
  24.5 1.8 %constant_dynamic-update-slice_fusion.14 = bf16[1536,1536]{1,0:T(8,128)(2,1)S(1)} fusion(bf16[1536,768]{1,0:T(8,128)(2,1)} %param.5), kind=kLoop, calls=%fused_computation.83 | loop fusion | bytes 4718592
  26.4 0.6 collective-permute-start.10
  27.0 0.2 constant_dynamic-update-slice_fusion.16
  27.2 0.0 collective-permute-done.5
  27.2 3.4 %collective-permute-done.4 = bf16[32,3072]{1,0:T(8,128)(2,1)S(1)} collective-permute-done((bf16[32,3072]{1,0:T(8,128)(2,1)S(1)}, bf16[32,3072]{1,0:T(8,128)(2,1)S(1)}, u32[]{:S(2)}, u32[]{:S(2)}) %collective-permute-start.4) | collective-permute-done | bytes 196640 | tf_op jit(solution)/shard_map/ppermute | solution.py:45
  30.5 5.4 %collective-permute-start.8 = (bf16[32,3072]{1,0:T(8,128)(2,1)S(1)}, bf16[32,3072]{1,0:T(8,128)(2,1)S(1)}, u32[]{:S(2)}, u32[]{:S(2)}) collective-permute-start(bf16[32,3072]{1,0:T(8,128)(2,1)S(1)} %collective-permute-done.4), channel_id=1, source_target_pairs={{0,30},{1,19},{2,20},{3,17},{4,18},{5,23},{6,24},{7,21},{8,22},{9,... | collective-permute-start | bytes 589832 | tf_op jit(solution)/shard_map/ppermute | solution.py:45
  35.9 1.2 collective-permute-start.7
  37.2 0.0 collective-permute-done.6
  37.2 5.7 %collective-permute-done.7 = bf16[32,3072]{1,0:T(8,128)(2,1)S(1)} collective-permute-done((bf16[32,3072]{1,0:T(8,128)(2,1)S(1)}, bf16[32,3072]{1,0:T(8,128)(2,1)S(1)}, u32[]{:S(2)}, u32[]{:S(2)}) %collective-permute-start.7) | collective-permute-done | bytes 196640 | tf_op jit(solution)/shard_map/ppermute | solution.py:45
  42.9 0.2 constant_dynamic-update-slice_fusion.13
  43.1 1.4 %convolution_convert_fusion.1 = bf16[256,1536]{1,0:T(8,128)(2,1)S(1)} fusion(bf16[1536,1536]{1,0:T(8,128)(2,1)S(1)} %constant_dynamic-update-slice_fusion.13, bf16[256,3072]{1,0:T(8,128)(2,1)S(1)} %constant_dynamic-update-slice_fusion.2), kind=kOutput, calls=%fused_computation.18 | convolution fusion | flops 1208352768 | bytes 6291456 | tf_op jit(solution)/shard_map/dot_general | solution.py:76
  44.5 0.2 constant_dynamic-update-slice_fusion.15
  44.7 1.4 %convolution_convert_fusion = bf16[256,1536]{1,0:T(8,128)(2,1)S(1)} fusion(bf16[1536,1536]{1,0:T(8,128)(2,1)S(1)} %constant_dynamic-update-slice_fusion.15, bf16[256,3072]{1,0:T(8,128)(2,1)S(1)} %constant_dynamic-update-slice_fusion.2), kind=kOutput, calls=%fused_computation.17 | convolution fusion | flops 1208352768 | bytes 6291456 | tf_op jit(solution)/shard_map/dot_general | solution.py:77
  46.1 0.2 pad_maximum_fusion.1
  46.3 20.1 %all_to_all.10 = bf16[8,2,32,1536]{3,2,1,0:T(8,128)(2,1)S(1)} all-to-all(bf16[8,2,32,1536]{3,2,1,0:T(8,128)(2,1)S(1)} %pad_maximum_fusion.1), channel_id=1, replica_groups=mesh['row'=8,'col'=32] {'row'}, dimensions={0} | all-to-all | bytes 3145728 | tf_op jit(solution)/shard_map/all_to_all | solution.py:83
  66.4 0.2 convert_reduce_fusion
  66.6 0.1 multiply_convert_fusion.2
  66.7 0.1 broadcast_in_dim.2
  66.9 18.4 %all_to_all.11 = bf16[8,2,32,1536]{3,2,1,0:T(8,128)(2,1)S(1)} all-to-all(bf16[8,2,32,1536]{3,2,1,0:T(8,128)(2,1)S(1)} %broadcast_in_dim.2), channel_id=1, replica_groups=mesh['row'=8,'col'=32] {'row'}, dimensions={0} | all-to-all | bytes 3145728 | tf_op jit(solution)/shard_map/all_to_all | solution.py:87
  85.3 0.1 fusion.32
  85.4 1.4 %fusion.35 = f32[256,1536]{1,0:T(8,128)S(1)} fusion(bf16[256,1536]{1,0:T(8,128)(2,1)S(1)} %bitcast.27, bf16[1536,1536]{1,0:T(8,128)(2,1)S(1)} %constant_dynamic-update-slice_fusion.13), kind=kOutput, calls=%fused_computation.90 | convolution fusion | flops 1207959552 | bytes 7077888 | tf_op jit(solution)/shard_map/dot_general | solution.py:94
  86.8 1.4 %fusion.34 = f32[256,1536]{1,0:T(8,128)S(1)} fusion(bf16[256,1536]{1,0:T(8,128)(2,1)S(1)} %bitcast.24, bf16[1536,1536]{1,0:T(8,128)(2,1)S(1)} %constant_dynamic-update-slice_fusion.15), kind=kOutput, calls=%fused_computation.89 | convolution fusion | flops 1207959552 | bytes 7077888 | tf_op jit(solution)/shard_map/dot_general | solution.py:93
  88.2 0.1 fusion.19
  88.3 0.2 fusion
  88.5 0.1 fusion.31
  88.6 2.2 %collective-permute-start.11 = (bf16[32,3072]{1,0:T(8,128)(2,1)S(1)}, bf16[32,3072]{1,0:T(8,128)(2,1)S(1)}, u32[]{:S(2)}, u32[]{:S(2)}) collective-permute-start(bf16[32,3072]{1,0:T(8,128)(2,1)S(1)} %pad_maximum_fusion.7), channel_id=1, source_target_pairs={{0,18},{1,31},{2,16},{3,21},{4,22},{5,19},{6,20},{7,25},{8,26},{9,... | collective-permute-start | bytes 589832 | tf_op jit(solution)/shard_map/ppermute | solution.py:45
  90.8 0.4 collective-permute-start.14
  91.2 0.8 fusion.7
  92.1 6.7 %collective-permute-done.11 = bf16[32,3072]{1,0:T(8,128)(2,1)S(1)} collective-permute-done((bf16[32,3072]{1,0:T(8,128)(2,1)S(1)}, bf16[32,3072]{1,0:T(8,128)(2,1)S(1)}, u32[]{:S(2)}, u32[]{:S(2)}) %collective-permute-start.11) | collective-permute-done | bytes 196640 | tf_op jit(solution)/shard_map/ppermute | solution.py:45
  98.8 3.0 %collective-permute-start.12 = (bf16[32,3072]{1,0:T(8,128)(2,1)S(1)}, bf16[32,3072]{1,0:T(8,128)(2,1)S(1)}, u32[]{:S(2)}, u32[]{:S(2)}) collective-permute-start(bf16[32,3072]{1,0:T(8,128)(2,1)S(1)} %pad_maximum_fusion.6), channel_id=1, source_target_pairs={{0,30},{1,19},{2,20},{3,17},{4,18},{5,23},{6,24},{7,21},{8,22},{9,... | collective-permute-start | bytes 589832 | tf_op jit(solution)/shard_map/ppermute | solution.py:45
  101.8 0.1 fusion.12
  101.8 1.6 %collective-permute-start.15 = (bf16[32,3072]{1,0:T(8,128)(2,1)S(1)}, bf16[32,3072]{1,0:T(8,128)(2,1)S(1)}, u32[]{:S(2)}, u32[]{:S(2)}) collective-permute-start(bf16[32,3072]{1,0:T(8,128)(2,1)S(1)} %fusion.12), channel_id=1, source_target_pairs={{0,14},{1,3},{2,4},{3,1},{4,2},{5,7},{6,8},{7,5},{8,6},{9,11},{10,... | collective-permute-start | bytes 589832 | tf_op jit(solution)/shard_map/ppermute | solution.py:45
  103.5 0.1 slice_bitcast_fusion.4
  103.5 0.1 pad_maximum_fusion.2
  103.6 0.1 collective-permute-start.20
  103.7 0.5 collective-permute-start.21
  104.2 3.8 %collective-permute-done.12 = bf16[32,3072]{1,0:T(8,128)(2,1)S(1)} collective-permute-done((bf16[32,3072]{1,0:T(8,128)(2,1)S(1)}, bf16[32,3072]{1,0:T(8,128)(2,1)S(1)}, u32[]{:S(2)}, u32[]{:S(2)}) %collective-permute-start.12) | collective-permute-done | bytes 196640 | tf_op jit(solution)/shard_map/ppermute | solution.py:45
  108.1 1.0 collective-permute-start.13
  109.0 0.0 collective-permute-done.15
  109.0 0.1 fusion.11
  109.1 1.7 %collective-permute-start.16 = (bf16[32,3072]{1,0:T(8,128)(2,1)S(1)}, bf16[32,3072]{1,0:T(8,128)(2,1)S(1)}, u32[]{:S(2)}, u32[]{:S(2)}) collective-permute-start(bf16[32,3072]{1,0:T(8,128)(2,1)S(1)} %fusion.11), channel_id=1, source_target_pairs={{0,2},{1,15},{2,0},{3,5},{4,6},{5,3},{6,4},{7,9},{8,10},{9,7},{10,... | collective-permute-start | bytes 589832 | tf_op jit(solution)/shard_map/ppermute | solution.py:45
  110.8 0.8 fusion.5
  111.6 2.5 %collective-permute-start.17 = (bf16[16,3072]{1,0:T(8,128)(2,1)S(1)}, bf16[16,3072]{1,0:T(8,128)(2,1)S(1)}, u32[]{:S(2)}, u32[]{:S(2)}) collective-permute-start(bf16[16,3072]{1,0:T(8,128)(2,1)S(1)} %get-tuple-element.35), channel_id=1, source_target_pairs={{0,16},{1,17},{2,18},{3,19},{4,20},{5,21},{6,22},{7,23},{8,24},{9,... | collective-permute-start | bytes 294920 | tf_op jit(solution)/shard_map/ppermute | solution.py:45
  114.1 2.1 %collective-permute-done.13 = bf16[32,3072]{1,0:T(8,128)(2,1)S(1)} collective-permute-done((bf16[32,3072]{1,0:T(8,128)(2,1)S(1)}, bf16[32,3072]{1,0:T(8,128)(2,1)S(1)}, u32[]{:S(2)}, u32[]{:S(2)}) %collective-permute-start.13) | collective-permute-done | bytes 196640 | tf_op jit(solution)/shard_map/ppermute | solution.py:45
  116.2 3.0 %collective-permute-start.18 = (bf16[16,3072]{1,0:T(8,128)(2,1)S(1)}, bf16[16,3072]{1,0:T(8,128)(2,1)S(1)}, u32[]{:S(2)}, u32[]{:S(2)}) collective-permute-start(bf16[16,3072]{1,0:T(8,128)(2,1)S(1)} %get-tuple-element.36), channel_id=1, source_target_pairs={{0,30},{1,19},{2,20},{3,17},{4,18},{5,23},{6,24},{7,21},{8,22},{9,... | collective-permute-start | bytes 294920 | tf_op jit(solution)/shard_map/ppermute | solution.py:45
  119.2 0.1 fusion.9
  119.3 0.9 collective-permute-start.19
  120.2 2.2 %multiply_convert_fusion.1 = bf16[768,1536]{1,0:T(8,128)(2,1)} fusion(f32[768,1536]{1,0:T(8,128)S(1)} %fusion.7, bf16[256,3072]{1,0:T(8,128)(2,1)S(1)} %collective-permute-done.21, bf16[2,256,768]{2,1,0:T(8,128)(2,1)S(1)} %collective-permute-done.20), kind=kOutput, calls=%fused_computation.14 | convolution fusion | flops 607518720 | bytes 8257536 | tf_op jit(solution)/shard_map/dot_general | solution.py:125
  122.4 2.2 %multiply_convert_fusion = bf16[1536,768]{1,0:T(8,128)(2,1)} fusion(f32[1536,768]{1,0:T(8,128)S(1)} %fusion.5, bf16[256,3072]{1,0:T(8,128)(2,1)S(1)} %collective-permute-done.21, bf16[2,256,768]{2,1,0:T(8,128)(2,1)S(1)} %collective-permute-done.20), kind=kOutput, calls=%fused_computation.13 | convolution fusion | flops 607518720 | bytes 8257536 | tf_op jit(solution)/shard_map/dot_general | solution.py:122
  124.6 0.6 collective-permute-done.19
  125.3 0.6 fusion.33
  (29 shorter events, 0.3 us)
Async XLA Ops:
  2.2 5.0 %collective-permute-start = (bf16[16,3072]{1,0:T(8,128)(2,1)S(1)}, bf16[16,3072]{1,0:T(8,128)(2,1)S(1)}, u32[]{:S(2)}, u32[]{:S(2)}) collective-permute-start(bf16[16,3072]{1,0:T(8,128)(2,1)S(1)} %get-tuple-element.66), channel_id=1, source_target_pairs={{0,2},{1,15},{2,0},{3,5},{4,6},{5,3},{6,4},{7,9},{8,10},{9,7},{10,... | collective-permute-start | bytes 294920 | tf_op jit(solution)/shard_map/ppermute | solution.py:45
  4.2 11.5 %collective-permute-start.3 = (bf16[16,3072]{1,0:T(8,128)(2,1)S(1)}, bf16[16,3072]{1,0:T(8,128)(2,1)S(1)}, u32[]{:S(2)}, u32[]{:S(2)}) collective-permute-start(bf16[16,3072]{1,0:T(8,128)(2,1)S(1)} %get-tuple-element.66), channel_id=1, source_target_pairs={{0,18},{1,31},{2,16},{3,21},{4,22},{5,19},{6,20},{7,25},{8,26},{9,... | collective-permute-start | bytes 294920 | tf_op jit(solution)/shard_map/ppermute | solution.py:45
  6.7 9.0 %collective-permute-start.2 = (bf16[16,3072]{1,0:T(8,128)(2,1)S(1)}, bf16[16,3072]{1,0:T(8,128)(2,1)S(1)}, u32[]{:S(2)}, u32[]{:S(2)}) collective-permute-start(bf16[16,3072]{1,0:T(8,128)(2,1)S(1)} %get-tuple-element.66), channel_id=1, source_target_pairs={{0,16},{1,17},{2,18},{3,19},{4,20},{5,21},{6,22},{7,23},{8,24},{9,... | collective-permute-start | bytes 294920 | tf_op jit(solution)/shard_map/ppermute | solution.py:45
  7.3 19.9 %collective-permute-start.5 = (bf16[32,3072]{1,0:T(8,128)(2,1)S(1)}, bf16[32,3072]{1,0:T(8,128)(2,1)S(1)}, u32[]{:S(2)}, u32[]{:S(2)}) collective-permute-start(bf16[32,3072]{1,0:T(8,128)(2,1)S(1)} %pad_maximum_fusion.3), channel_id=1, source_target_pairs={{0,30},{1,19},{2,20},{3,17},{4,18},{5,23},{6,24},{7,21},{8,22},{9,... | collective-permute-start | bytes 589832 | tf_op jit(solution)/shard_map/ppermute | solution.py:45
  15.7 6.9 %collective-permute-start.1 = (bf16[32,3072]{1,0:T(8,128)(2,1)S(1)}, bf16[32,3072]{1,0:T(8,128)(2,1)S(1)}, u32[]{:S(2)}, u32[]{:S(2)}) collective-permute-start(bf16[32,3072]{1,0:T(8,128)(2,1)S(1)} %pad_maximum_fusion.3), channel_id=1, source_target_pairs={{0,14},{1,3},{2,4},{3,1},{4,2},{5,7},{6,8},{7,5},{8,6},{9,11},{10,... | collective-permute-start | bytes 589832 | tf_op jit(solution)/shard_map/ppermute | solution.py:45
  15.7 10.7 %copy-start = (bf16[768,1536]{1,0:T(8,128)(2,1)S(1)}, bf16[768,1536]{1,0:T(8,128)(2,1)}, u32[]{:S(2)}) copy-start(bf16[768,1536]{1,0:T(8,128)(2,1)} %param.6) | copy-start | bytes 7077892
  22.5 14.6 %collective-permute-start.6 = (bf16[32,3072]{1,0:T(8,128)(2,1)S(1)}, bf16[32,3072]{1,0:T(8,128)(2,1)S(1)}, u32[]{:S(2)}, u32[]{:S(2)}) collective-permute-start(bf16[32,3072]{1,0:T(8,128)(2,1)S(1)} %collective-permute-done.1), channel_id=1, source_target_pairs={{0,18},{1,31},{2,16},{3,21},{4,22},{5,19},{6,20},{7,25},{8,26},{9,... | collective-permute-start | bytes 589832 | tf_op jit(solution)/shard_map/ppermute | solution.py:45
  22.5 8.0 %collective-permute-start.4 = (bf16[32,3072]{1,0:T(8,128)(2,1)S(1)}, bf16[32,3072]{1,0:T(8,128)(2,1)S(1)}, u32[]{:S(2)}, u32[]{:S(2)}) collective-permute-start(bf16[32,3072]{1,0:T(8,128)(2,1)S(1)} %collective-permute-done.1), channel_id=1, source_target_pairs={{0,2},{1,15},{2,0},{3,5},{4,6},{5,3},{6,4},{7,9},{8,10},{9,7},{10,... | collective-permute-start | bytes 589832 | tf_op jit(solution)/shard_map/ppermute | solution.py:45
  24.5 18.4 %collective-permute-start.9 = (bf16[1536,768]{1,0:T(8,128)(2,1)}, bf16[1536,768]{1,0:T(8,128)(2,1)S(1)}, u32[]{:S(2)}, u32[]{:S(2)}) collective-permute-start(bf16[1536,768]{1,0:T(8,128)(2,1)} %param.5), channel_id=1, source_target_pairs={{0,1},{1,0},{2,3},{3,2},{4,5},{5,4},{6,7},{7,6},{8,9},{9,8},{10,11... | collective-permute-start | bytes 7077896 | tf_op jit(solution)/shard_map/ppermute | solution.py:45
  26.4 18.1 %collective-permute-start.10 = (bf16[768,1536]{1,0:T(8,128)(2,1)S(1)}, bf16[768,1536]{1,0:T(8,128)(2,1)S(1)}, u32[]{:S(2)}, u32[]{:S(2)}) collective-permute-start(bf16[768,1536]{1,0:T(8,128)(2,1)S(1)} %copy-done), channel_id=1, source_target_pairs={{0,1},{1,0},{2,3},{3,2},{4,5},{5,4},{6,7},{7,6},{8,9},{9,8},{10,11... | collective-permute-start | bytes 7077896 | tf_op jit(solution)/shard_map/ppermute | solution.py:45
  30.5 12.3 %collective-permute-start.8 = (bf16[32,3072]{1,0:T(8,128)(2,1)S(1)}, bf16[32,3072]{1,0:T(8,128)(2,1)S(1)}, u32[]{:S(2)}, u32[]{:S(2)}) collective-permute-start(bf16[32,3072]{1,0:T(8,128)(2,1)S(1)} %collective-permute-done.4), channel_id=1, source_target_pairs={{0,30},{1,19},{2,20},{3,17},{4,18},{5,23},{6,24},{7,21},{8,22},{9,... | collective-permute-start | bytes 589832 | tf_op jit(solution)/shard_map/ppermute | solution.py:45
  35.9 7.0 %collective-permute-start.7 = (bf16[32,3072]{1,0:T(8,128)(2,1)S(1)}, bf16[32,3072]{1,0:T(8,128)(2,1)S(1)}, u32[]{:S(2)}, u32[]{:S(2)}) collective-permute-start(bf16[32,3072]{1,0:T(8,128)(2,1)S(1)} %collective-permute-done.4), channel_id=1, source_target_pairs={{0,14},{1,3},{2,4},{3,1},{4,2},{5,7},{6,8},{7,5},{8,6},{9,11},{10,... | collective-permute-start | bytes 589832 | tf_op jit(solution)/shard_map/ppermute | solution.py:45
  88.6 10.2 %collective-permute-start.11 = (bf16[32,3072]{1,0:T(8,128)(2,1)S(1)}, bf16[32,3072]{1,0:T(8,128)(2,1)S(1)}, u32[]{:S(2)}, u32[]{:S(2)}) collective-permute-start(bf16[32,3072]{1,0:T(8,128)(2,1)S(1)} %pad_maximum_fusion.7), channel_id=1, source_target_pairs={{0,18},{1,31},{2,16},{3,21},{4,22},{5,19},{6,20},{7,25},{8,26},{9,... | collective-permute-start | bytes 589832 | tf_op jit(solution)/shard_map/ppermute | solution.py:45
  90.8 11.0 %collective-permute-start.14 = (bf16[32,3072]{1,0:T(8,128)(2,1)S(1)}, bf16[32,3072]{1,0:T(8,128)(2,1)S(1)}, u32[]{:S(2)}, u32[]{:S(2)}) collective-permute-start(bf16[32,3072]{1,0:T(8,128)(2,1)S(1)} %pad_maximum_fusion.8), channel_id=1, source_target_pairs={{0,2},{1,15},{2,0},{3,5},{4,6},{5,3},{6,4},{7,9},{8,10},{9,7},{10,... | collective-permute-start | bytes 589832 | tf_op jit(solution)/shard_map/ppermute | solution.py:45
  98.8 9.3 %collective-permute-start.12 = (bf16[32,3072]{1,0:T(8,128)(2,1)S(1)}, bf16[32,3072]{1,0:T(8,128)(2,1)S(1)}, u32[]{:S(2)}, u32[]{:S(2)}) collective-permute-start(bf16[32,3072]{1,0:T(8,128)(2,1)S(1)} %pad_maximum_fusion.6), channel_id=1, source_target_pairs={{0,30},{1,19},{2,20},{3,17},{4,18},{5,23},{6,24},{7,21},{8,22},{9,... | collective-permute-start | bytes 589832 | tf_op jit(solution)/shard_map/ppermute | solution.py:45
  101.8 7.2 %collective-permute-start.15 = (bf16[32,3072]{1,0:T(8,128)(2,1)S(1)}, bf16[32,3072]{1,0:T(8,128)(2,1)S(1)}, u32[]{:S(2)}, u32[]{:S(2)}) collective-permute-start(bf16[32,3072]{1,0:T(8,128)(2,1)S(1)} %fusion.12), channel_id=1, source_target_pairs={{0,14},{1,3},{2,4},{3,1},{4,2},{5,7},{6,8},{7,5},{8,6},{9,11},{10,... | collective-permute-start | bytes 589832 | tf_op jit(solution)/shard_map/ppermute | solution.py:45
  103.6 16.5 %collective-permute-start.20 = (bf16[2,256,768]{2,1,0:T(8,128)(2,1)S(1)}, bf16[2,256,768]{2,1,0:T(8,128)(2,1)S(1)}, u32[]{:S(2)}, u32[]{:S(2)}) collective-permute-start(bf16[2,256,768]{2,1,0:T(8,128)(2,1)S(1)} %pad_maximum_fusion.2), channel_id=1, source_target_pairs={{0,1},{1,0},{2,3},{3,2},{4,5},{5,4},{6,7},{7,6},{8,9},{9,8},{10,11... | collective-permute-start | bytes 2359304 | tf_op jit(solution)/shard_map/ppermute | solution.py:45
  103.7 16.4 %collective-permute-start.21 = (bf16[256,3072]{1,0:T(8,128)(2,1)S(1)}, bf16[256,3072]{1,0:T(8,128)(2,1)S(1)}, u32[]{:S(2)}, u32[]{:S(2)}) collective-permute-start(bf16[256,3072]{1,0:T(8,128)(2,1)S(1)} %constant_dynamic-update-slice_fusion.2), channel_id=1, source_target_pairs={{0,1},{1,0},{2,3},{3,2},{4,5},{5,4},{6,7},{7,6},{8,9},{9,8},{10,11... | collective-permute-start | bytes 4718600 | tf_op jit(solution)/shard_map/ppermute | solution.py:45
  108.1 8.2 %collective-permute-start.13 = (bf16[32,3072]{1,0:T(8,128)(2,1)S(1)}, bf16[32,3072]{1,0:T(8,128)(2,1)S(1)}, u32[]{:S(2)}, u32[]{:S(2)}) collective-permute-start(bf16[32,3072]{1,0:T(8,128)(2,1)S(1)} %pad_maximum_fusion.5), channel_id=1, source_target_pairs={{0,18},{1,31},{2,16},{3,21},{4,22},{5,19},{6,20},{7,25},{8,26},{9,... | collective-permute-start | bytes 589832 | tf_op jit(solution)/shard_map/ppermute | solution.py:45
  109.1 10.1 %collective-permute-start.16 = (bf16[32,3072]{1,0:T(8,128)(2,1)S(1)}, bf16[32,3072]{1,0:T(8,128)(2,1)S(1)}, u32[]{:S(2)}, u32[]{:S(2)}) collective-permute-start(bf16[32,3072]{1,0:T(8,128)(2,1)S(1)} %fusion.11), channel_id=1, source_target_pairs={{0,2},{1,15},{2,0},{3,5},{4,6},{5,3},{6,4},{7,9},{8,10},{9,7},{10,... | collective-permute-start | bytes 589832 | tf_op jit(solution)/shard_map/ppermute | solution.py:45
  111.6 13.6 %collective-permute-start.17 = (bf16[16,3072]{1,0:T(8,128)(2,1)S(1)}, bf16[16,3072]{1,0:T(8,128)(2,1)S(1)}, u32[]{:S(2)}, u32[]{:S(2)}) collective-permute-start(bf16[16,3072]{1,0:T(8,128)(2,1)S(1)} %get-tuple-element.35), channel_id=1, source_target_pairs={{0,16},{1,17},{2,18},{3,19},{4,20},{5,21},{6,22},{7,23},{8,24},{9,... | collective-permute-start | bytes 294920 | tf_op jit(solution)/shard_map/ppermute | solution.py:45
  116.2 9.0 %collective-permute-start.18 = (bf16[16,3072]{1,0:T(8,128)(2,1)S(1)}, bf16[16,3072]{1,0:T(8,128)(2,1)S(1)}, u32[]{:S(2)}, u32[]{:S(2)}) collective-permute-start(bf16[16,3072]{1,0:T(8,128)(2,1)S(1)} %get-tuple-element.36), channel_id=1, source_target_pairs={{0,30},{1,19},{2,20},{3,17},{4,18},{5,23},{6,24},{7,21},{8,22},{9,... | collective-permute-start | bytes 294920 | tf_op jit(solution)/shard_map/ppermute | solution.py:45
  119.3 5.9 %collective-permute-start.19 = (bf16[16,3072]{1,0:T(8,128)(2,1)S(1)}, bf16[16,3072]{1,0:T(8,128)(2,1)S(1)}, u32[]{:S(2)}, u32[]{:S(2)}) collective-permute-start(bf16[16,3072]{1,0:T(8,128)(2,1)S(1)} %slice.267), channel_id=1, source_target_pairs={{0,14},{1,3},{2,4},{3,1},{4,2},{5,7},{6,8},{7,5},{8,6},{9,11},{10,... | collective-permute-start | bytes 294920 | tf_op jit(solution)/shard_map/ppermute | solution.py:45

commit v4 on v3

--- a/solution.py
+++ b/solution.py
@@ -108,8 +108,7 @@
     near2, far2 = rows_of(1, 8), rows_of(3, 10)
     near3, far3 = rows_of(5, 12), rows_of(7, 14)
     near4, far4 = rows_of(9, 13), rows_of(11, 15)
-    far4 = moved(far4, even[1])
-    near3 = near3 + far4 + moved(near4, even[0])
+    near3 = near3 + moved(far4, even[1]) + moved(near4, even[0])
 
     acts_sent = jnp.stack([hidden[:, hid:], grad_pre[:, hid:]])
     acts_other = swap(after(acts_sent, near3), swap_core)
@@ -128,13 +127,12 @@
     grad_up = (grad_up * grad_scale).astype(jnp.bfloat16)
     grad_down = (grad_down * grad_scale).astype(jnp.bfloat16)
 
-    far3 = moved(far3, odd[1], far4)
-    near2 = near2 + far3 + moved(near3, odd[0])
-    far2 = moved(far2, even[1], far3)
-    far0 = moved(far01[:share], swap_half, far4)
-    far1 = moved(far01[share:], odd[1], far3)
-    near01 = near01 + far2 + moved(near2, even[0])
-    acc = near01[:share] + far0 + far1
+    far2 = far2 + moved(far3, odd[0])
+    near2 = near2 + moved(near3, odd[0])
+    far01 = far01 + moved(far2, even[0])
+    near01 = near01 + moved(near2, even[0])
+    far0 = far01[:share] + moved(far01[share:], odd[0])
+    acc = near01[:share] + moved(far0, swap_half)
     near1 = moved(near01[share:], odd[0])
     near1, grad_down = lax.optimization_barrier((near1, grad_down))
     near1, grad_up = lax.optimization_barrier((near1, grad_up))

time: 127 us -> 126 us (level)
  starting transfers between devices: 39.4 us -> 32.3 us
  waiting for transfers between devices: 29.1 us -> 35.5 us
    ppermute x22, starting transfers between devices: 39.4 us -> 32.3 us  [swap(): return lax.ppermute(value, 'col', perm)]
    ppermute x22, waiting for transfers between devices: 29.1 us -> 35.5 us  [swap(): return lax.ppermute(value, 'col', perm)]
  transfers between devices with their start and end apart: 22 -> 22, of which waited for: 7 -> 11; matrix products, arithmetic and copies ran while one was open for 8% -> 7% of each run, Pallas kernels for 0% -> 0%
where the time goes in v4:
time: 126 us; the launch traced here: 125 us
  blocking collectives  38.4 us (30%)
  waiting for transfers between devices  35.5 us (28%)
  starting transfers between devices  32.3 us (26%)
  matrix products  11.7 us (9%)
  local copies, waits for them, and re-layouts  5.09 us (4%)
  other arithmetic  1.31 us (1%)
    ppermute x22, waiting for transfers between devices, swap(): return lax.ppermute(value, 'col', perm)  35.5 us
    ppermute x22, starting transfers between devices, swap(): return lax.ppermute(value, 'col', perm)  32.3 us
    all_to_all x1, blocking collectives, local(): parts = lax.all_to_all(parts, 'row', 0, 0)  20.1 us
    all_to_all x1, blocking collectives, local(): lax.all_to_all(jnp.broadcast_to(pair[None], (rows,) + pair.shape), 'row',...  18.4 us
    dot_general x2, matrix products, local(): lax.dot_general(tok[:, :feats], g, contract_first, preferred_element_type...  3.08 us
    dot_general x2, matrix products, local(): lax.dot_general(h, tok[:, feats:], contract_first, preferred_element_type...  3.03 us
    unnamed x13, local copies, waits for them, and re-layouts  2.9 us
  transfers between devices with their start and end apart: 22, of which 11 were waited for; matrix products, arithmetic and copies ran while one was open for 7% of the time, Pallas kernels for 0%

profile of v4, /device:TPU:8, one launch (start us, length us, event | category | flops | bytes accessed | tf_op | source)
XLA Modules:
  0.0 125.4 jit_solution(2905591268361953609)
XLA Ops:
  0.6 0.8 constant_dynamic-update-slice_fusion.1
  1.4 0.8 constant_dynamic-update-slice_fusion
  2.2 1.9 %collective-permute-start = (bf16[16,3072]{1,0:T(8,128)(2,1)S(1)}, bf16[16,3072]{1,0:T(8,128)(2,1)S(1)}, u32[]{:S(2)}, u32[]{:S(2)}) collective-permute-start(bf16[16,3072]{1,0:T(8,128)(2,1)S(1)} %get-tuple-element.57), channel_id=1, source_target_pairs={{0,2},{1,15},{2,0},{3,5},{4,6},{5,3},{6,4},{7,9},{8,10},{9,7},{10,... | collective-permute-start | bytes 294920 | tf_op jit(solution)/shard_map/ppermute | solution.py:45
  4.2 2.6 %collective-permute-start.3 = (bf16[16,3072]{1,0:T(8,128)(2,1)S(1)}, bf16[16,3072]{1,0:T(8,128)(2,1)S(1)}, u32[]{:S(2)}, u32[]{:S(2)}) collective-permute-start(bf16[16,3072]{1,0:T(8,128)(2,1)S(1)} %get-tuple-element.57), channel_id=1, source_target_pairs={{0,18},{1,31},{2,16},{3,21},{4,22},{5,19},{6,20},{7,25},{8,26},{9,... | collective-permute-start | bytes 294920 | tf_op jit(solution)/shard_map/ppermute | solution.py:45
  6.7 0.5 collective-permute-start.2
  7.3 8.4 %collective-permute-start.5 = (bf16[32,3072]{1,0:T(8,128)(2,1)S(1)}, bf16[32,3072]{1,0:T(8,128)(2,1)S(1)}, u32[]{:S(2)}, u32[]{:S(2)}) collective-permute-start(bf16[32,3072]{1,0:T(8,128)(2,1)S(1)} %pad_maximum_fusion.3), channel_id=1, source_target_pairs={{0,30},{1,19},{2,20},{3,17},{4,18},{5,23},{6,24},{7,21},{8,22},{9,... | collective-permute-start | bytes 589832 | tf_op jit(solution)/shard_map/ppermute | solution.py:45
  15.7 0.0 collective-permute-start.1
  15.7 0.0 copy-start
  15.7 6.8 %collective-permute-done.1 = bf16[32,3072]{1,0:T(8,128)(2,1)S(1)} collective-permute-done((bf16[32,3072]{1,0:T(8,128)(2,1)S(1)}, bf16[32,3072]{1,0:T(8,128)(2,1)S(1)}, u32[]{:S(2)}, u32[]{:S(2)}) %collective-permute-start.1) | collective-permute-done | bytes 196640 | tf_op jit(solution)/shard_map/ppermute | solution.py:45
  22.5 2.0 %collective-permute-start.4 = (bf16[32,3072]{1,0:T(8,128)(2,1)S(1)}, bf16[32,3072]{1,0:T(8,128)(2,1)S(1)}, u32[]{:S(2)}, u32[]{:S(2)}) collective-permute-start(bf16[32,3072]{1,0:T(8,128)(2,1)S(1)} %collective-permute-done.1), channel_id=1, source_target_pairs={{0,2},{1,15},{2,0},{3,5},{4,6},{5,3},{6,4},{7,9},{8,10},{9,7},{10,... | collective-permute-start | bytes 589832 | tf_op jit(solution)/shard_map/ppermute | solution.py:45
  24.5 0.0 collective-permute-start.9
  24.5 1.8 %constant_dynamic-update-slice_fusion.14 = bf16[1536,1536]{1,0:T(8,128)(2,1)S(1)} fusion(bf16[1536,768]{1,0:T(8,128)(2,1)} %param.5), kind=kLoop, calls=%fused_computation.97 | loop fusion | bytes 4718592
  26.4 0.6 collective-permute-start.10
  27.0 0.2 constant_dynamic-update-slice_fusion.16
  27.2 3.4 %collective-permute-done.4 = bf16[32,3072]{1,0:T(8,128)(2,1)S(1)} collective-permute-done((bf16[32,3072]{1,0:T(8,128)(2,1)S(1)}, bf16[32,3072]{1,0:T(8,128)(2,1)S(1)}, u32[]{:S(2)}, u32[]{:S(2)}) %collective-permute-start.4) | collective-permute-done | bytes 196640 | tf_op jit(solution)/shard_map/ppermute | solution.py:45
  30.5 5.4 %collective-permute-start.8 = (bf16[32,3072]{1,0:T(8,128)(2,1)S(1)}, bf16[32,3072]{1,0:T(8,128)(2,1)S(1)}, u32[]{:S(2)}, u32[]{:S(2)}) collective-permute-start(bf16[32,3072]{1,0:T(8,128)(2,1)S(1)} %collective-permute-done.4), channel_id=1, source_target_pairs={{0,30},{1,19},{2,20},{3,17},{4,18},{5,23},{6,24},{7,21},{8,22},{9,... | collective-permute-start | bytes 589832 | tf_op jit(solution)/shard_map/ppermute | solution.py:45
  35.9 1.2 collective-permute-start.7
  37.2 0.0 collective-permute-done.6
  37.2 5.7 %collective-permute-done.7 = bf16[32,3072]{1,0:T(8,128)(2,1)S(1)} collective-permute-done((bf16[32,3072]{1,0:T(8,128)(2,1)S(1)}, bf16[32,3072]{1,0:T(8,128)(2,1)S(1)}, u32[]{:S(2)}, u32[]{:S(2)}) %collective-permute-start.7) | collective-permute-done | bytes 196640 | tf_op jit(solution)/shard_map/ppermute | solution.py:45
  42.9 0.0 collective-permute-done.8
  42.9 0.0 collective-permute-done.9
  42.9 0.2 constant_dynamic-update-slice_fusion.13
  43.1 1.4 %convolution_convert_fusion.1 = bf16[256,1536]{1,0:T(8,128)(2,1)S(1)} fusion(bf16[1536,1536]{1,0:T(8,128)(2,1)S(1)} %constant_dynamic-update-slice_fusion.13, bf16[256,3072]{1,0:T(8,128)(2,1)S(1)} %constant_dynamic-update-slice_fusion.2), kind=kOutput, calls=%fused_computation.26 | convolution fusion | flops 1208352768 | bytes 6291456 | tf_op jit(solution)/shard_map/dot_general | solution.py:76
  44.5 0.0 collective-permute-done.10
  44.5 0.2 constant_dynamic-update-slice_fusion.15
  44.7 1.4 %convolution_convert_fusion = bf16[256,1536]{1,0:T(8,128)(2,1)S(1)} fusion(bf16[1536,1536]{1,0:T(8,128)(2,1)S(1)} %constant_dynamic-update-slice_fusion.15, bf16[256,3072]{1,0:T(8,128)(2,1)S(1)} %constant_dynamic-update-slice_fusion.2), kind=kOutput, calls=%fused_computation.25 | convolution fusion | flops 1208352768 | bytes 6291456 | tf_op jit(solution)/shard_map/dot_general | solution.py:77
  46.1 0.2 pad_maximum_fusion.1
  46.3 20.1 %all_to_all.10 = bf16[8,2,32,1536]{3,2,1,0:T(8,128)(2,1)S(1)} all-to-all(bf16[8,2,32,1536]{3,2,1,0:T(8,128)(2,1)S(1)} %pad_maximum_fusion.1), channel_id=1, replica_groups=mesh['row'=8,'col'=32] {'row'}, dimensions={0} | all-to-all | bytes 3145728 | tf_op jit(solution)/shard_map/all_to_all | solution.py:83
  66.4 0.2 convert_reduce_fusion
  66.6 0.1 multiply_convert_fusion.2
  66.7 0.1 broadcast_in_dim.2
  66.9 18.4 %all_to_all.11 = bf16[8,2,32,1536]{3,2,1,0:T(8,128)(2,1)S(1)} all-to-all(bf16[8,2,32,1536]{3,2,1,0:T(8,128)(2,1)S(1)} %broadcast_in_dim.2), channel_id=1, replica_groups=mesh['row'=8,'col'=32] {'row'}, dimensions={0} | all-to-all | bytes 3145728 | tf_op jit(solution)/shard_map/all_to_all | solution.py:87
  85.3 0.1 fusion.35
  85.4 1.4 %fusion.38 = f32[256,1536]{1,0:T(8,128)S(1)} fusion(bf16[256,1536]{1,0:T(8,128)(2,1)S(1)} %bitcast.27, bf16[1536,1536]{1,0:T(8,128)(2,1)S(1)} %constant_dynamic-update-slice_fusion.13), kind=kOutput, calls=%fused_computation.104 | convolution fusion | flops 1207959552 | bytes 7077888 | tf_op jit(solution)/shard_map/dot_general | solution.py:94
  86.8 1.4 %fusion.37 = f32[256,1536]{1,0:T(8,128)S(1)} fusion(bf16[256,1536]{1,0:T(8,128)(2,1)S(1)} %bitcast.24, bf16[1536,1536]{1,0:T(8,128)(2,1)S(1)} %constant_dynamic-update-slice_fusion.15), kind=kOutput, calls=%fused_computation.103 | convolution fusion | flops 1207959552 | bytes 7077888 | tf_op jit(solution)/shard_map/dot_general | solution.py:93
  88.2 0.2 fusion
  88.4 0.1 fusion.22
  88.6 0.8 fusion.7
  89.4 0.8 fusion.5
  90.3 2.2 %collective-permute-start.15 = (bf16[32,3072]{1,0:T(8,128)(2,1)S(1)}, bf16[32,3072]{1,0:T(8,128)(2,1)S(1)}, u32[]{:S(2)}, u32[]{:S(2)}) collective-permute-start(bf16[32,3072]{1,0:T(8,128)(2,1)S(1)} %pad_maximum_fusion.7), channel_id=1, source_target_pairs={{0,14},{1,3},{2,4},{3,1},{4,2},{5,7},{6,8},{7,5},{8,6},{9,11},{10,... | collective-permute-start | bytes 589832 | tf_op jit(solution)/shard_map/ppermute | solution.py:45
  92.5 0.1 slice_bitcast_fusion.4
  92.6 1.3 %collective-permute-start.11 = (bf16[32,3072]{1,0:T(8,128)(2,1)S(1)}, bf16[32,3072]{1,0:T(8,128)(2,1)S(1)}, u32[]{:S(2)}, u32[]{:S(2)}) collective-permute-start(bf16[32,3072]{1,0:T(8,128)(2,1)S(1)} %pad_maximum_fusion.5), channel_id=1, source_target_pairs={{0,18},{1,31},{2,16},{3,21},{4,22},{5,19},{6,20},{7,25},{8,26},{9,... | collective-permute-start | bytes 589832 | tf_op jit(solution)/shard_map/ppermute | solution.py:45
  93.9 1.7 %collective-permute-start.12 = (bf16[32,3072]{1,0:T(8,128)(2,1)S(1)}, bf16[32,3072]{1,0:T(8,128)(2,1)S(1)}, u32[]{:S(2)}, u32[]{:S(2)}) collective-permute-start(bf16[32,3072]{1,0:T(8,128)(2,1)S(1)} %pad_maximum_fusion.6), channel_id=1, source_target_pairs={{0,2},{1,15},{2,0},{3,5},{4,6},{5,3},{6,4},{7,9},{8,10},{9,7},{10,... | collective-permute-start | bytes 589832 | tf_op jit(solution)/shard_map/ppermute | solution.py:45
  95.6 0.1 pad_maximum_fusion.2
  95.7 3.5 %collective-permute-done.15 = bf16[32,3072]{1,0:T(8,128)(2,1)S(1)} collective-permute-done((bf16[32,3072]{1,0:T(8,128)(2,1)S(1)}, bf16[32,3072]{1,0:T(8,128)(2,1)S(1)}, u32[]{:S(2)}, u32[]{:S(2)}) %collective-permute-start.15) | collective-permute-done | bytes 196640 | tf_op jit(solution)/shard_map/ppermute | solution.py:45
  99.2 0.1 collective-permute-start.16
  99.3 3.0 %collective-permute-done.11 = bf16[32,3072]{1,0:T(8,128)(2,1)S(1)} collective-permute-done((bf16[32,3072]{1,0:T(8,128)(2,1)S(1)}, bf16[32,3072]{1,0:T(8,128)(2,1)S(1)}, u32[]{:S(2)}, u32[]{:S(2)}) %collective-permute-start.11) | collective-permute-done | bytes 196640 | tf_op jit(solution)/shard_map/ppermute | solution.py:45
  102.3 1.1 collective-permute-done.12
  103.4 0.1 fusion.10
  103.5 0.8 collective-permute-start.13
  104.3 0.0 collective-permute-start.20
  104.3 0.5 collective-permute-start.21
  104.8 0.7 collective-permute-done.16
  105.6 1.9 %collective-permute-start.17 = (bf16[16,3072]{1,0:T(8,128)(2,1)S(1)}, bf16[16,3072]{1,0:T(8,128)(2,1)S(1)}, u32[]{:S(2)}, u32[]{:S(2)}) collective-permute-start(bf16[16,3072]{1,0:T(8,128)(2,1)S(1)} %slice.305), channel_id=1, source_target_pairs={{0,14},{1,3},{2,4},{3,1},{4,2},{5,7},{6,8},{7,5},{8,6},{9,11},{10,... | collective-permute-start | bytes 294920 | tf_op jit(solution)/shard_map/ppermute | solution.py:45
  107.5 4.4 %collective-permute-done.13 = bf16[32,3072]{1,0:T(8,128)(2,1)S(1)} collective-permute-done((bf16[32,3072]{1,0:T(8,128)(2,1)S(1)}, bf16[32,3072]{1,0:T(8,128)(2,1)S(1)}, u32[]{:S(2)}, u32[]{:S(2)}) %collective-permute-start.13) | collective-permute-done | bytes 196640 | tf_op jit(solution)/shard_map/ppermute | solution.py:45
  111.9 0.1 collective-permute-start.14
  112.0 1.6 %collective-permute-done.17 = bf16[16,3072]{1,0:T(8,128)(2,1)S(1)} collective-permute-done((bf16[16,3072]{1,0:T(8,128)(2,1)S(1)}, bf16[16,3072]{1,0:T(8,128)(2,1)S(1)}, u32[]{:S(2)}, u32[]{:S(2)}) %collective-permute-start.17) | collective-permute-done | bytes 98336 | tf_op jit(solution)/shard_map/ppermute | solution.py:45
  113.7 1.1 collective-permute-start.18
  114.7 4.0 %collective-permute-done.14 = bf16[32,3072]{1,0:T(8,128)(2,1)S(1)} collective-permute-done((bf16[32,3072]{1,0:T(8,128)(2,1)S(1)}, bf16[32,3072]{1,0:T(8,128)(2,1)S(1)}, u32[]{:S(2)}, u32[]{:S(2)}) %collective-permute-start.14) | collective-permute-done | bytes 196640 | tf_op jit(solution)/shard_map/ppermute | solution.py:45
  118.8 0.1 collective-permute-start.19
  118.9 2.2 %multiply_convert_fusion.1 = bf16[768,1536]{1,0:T(8,128)(2,1)} fusion(f32[768,1536]{1,0:T(8,128)S(1)} %fusion.7, bf16[256,3072]{1,0:T(8,128)(2,1)S(1)} %collective-permute-done.21, bf16[2,256,768]{2,1,0:T(8,128)(2,1)S(1)} %collective-permute-done.20), kind=kOutput, calls=%fused_computation.22 | convolution fusion | flops 607518720 | bytes 8257536 | tf_op jit(solution)/shard_map/dot_general | solution.py:124
  121.2 2.3 %multiply_convert_fusion = bf16[1536,768]{1,0:T(8,128)(2,1)} fusion(f32[1536,768]{1,0:T(8,128)S(1)} %fusion.5, bf16[256,3072]{1,0:T(8,128)(2,1)S(1)} %collective-permute-done.21, bf16[2,256,768]{2,1,0:T(8,128)(2,1)S(1)} %collective-permute-done.20), kind=kOutput, calls=%fused_computation.21 | convolution fusion | flops 607518720 | bytes 8257536 | tf_op jit(solution)/shard_map/dot_general | solution.py:121
  123.4 1.3 %collective-permute-done.19 = bf16[16,3072]{1,0:T(8,128)(2,1)S(1)} collective-permute-done((bf16[16,3072]{1,0:T(8,128)(2,1)S(1)}, bf16[16,3072]{1,0:T(8,128)(2,1)S(1)}, u32[]{:S(2)}, u32[]{:S(2)}) %collective-permute-start.19) | collective-permute-done | bytes 98336 | tf_op jit(solution)/shard_map/ppermute | solution.py:45
  124.8 0.6 fusion.36
  (33 shorter events, 0.5 us)
Async XLA Ops:
  2.2 5.0 %collective-permute-start = (bf16[16,3072]{1,0:T(8,128)(2,1)S(1)}, bf16[16,3072]{1,0:T(8,128)(2,1)S(1)}, u32[]{:S(2)}, u32[]{:S(2)}) collective-permute-start(bf16[16,3072]{1,0:T(8,128)(2,1)S(1)} %get-tuple-element.57), channel_id=1, source_target_pairs={{0,2},{1,15},{2,0},{3,5},{4,6},{5,3},{6,4},{7,9},{8,10},{9,7},{10,... | collective-permute-start | bytes 294920 | tf_op jit(solution)/shard_map/ppermute | solution.py:45
  4.2 11.5 %collective-permute-start.3 = (bf16[16,3072]{1,0:T(8,128)(2,1)S(1)}, bf16[16,3072]{1,0:T(8,128)(2,1)S(1)}, u32[]{:S(2)}, u32[]{:S(2)}) collective-permute-start(bf16[16,3072]{1,0:T(8,128)(2,1)S(1)} %get-tuple-element.57), channel_id=1, source_target_pairs={{0,18},{1,31},{2,16},{3,21},{4,22},{5,19},{6,20},{7,25},{8,26},{9,... | collective-permute-start | bytes 294920 | tf_op jit(solution)/shard_map/ppermute | solution.py:45
  6.7 9.0 %collective-permute-start.2 = (bf16[16,3072]{1,0:T(8,128)(2,1)S(1)}, bf16[16,3072]{1,0:T(8,128)(2,1)S(1)}, u32[]{:S(2)}, u32[]{:S(2)}) collective-permute-start(bf16[16,3072]{1,0:T(8,128)(2,1)S(1)} %get-tuple-element.57), channel_id=1, source_target_pairs={{0,16},{1,17},{2,18},{3,19},{4,20},{5,21},{6,22},{7,23},{8,24},{9,... | collective-permute-start | bytes 294920 | tf_op jit(solution)/shard_map/ppermute | solution.py:45
  7.3 19.9 %collective-permute-start.5 = (bf16[32,3072]{1,0:T(8,128)(2,1)S(1)}, bf16[32,3072]{1,0:T(8,128)(2,1)S(1)}, u32[]{:S(2)}, u32[]{:S(2)}) collective-permute-start(bf16[32,3072]{1,0:T(8,128)(2,1)S(1)} %pad_maximum_fusion.3), channel_id=1, source_target_pairs={{0,30},{1,19},{2,20},{3,17},{4,18},{5,23},{6,24},{7,21},{8,22},{9,... | collective-permute-start | bytes 589832 | tf_op jit(solution)/shard_map/ppermute | solution.py:45
  15.7 6.9 %collective-permute-start.1 = (bf16[32,3072]{1,0:T(8,128)(2,1)S(1)}, bf16[32,3072]{1,0:T(8,128)(2,1)S(1)}, u32[]{:S(2)}, u32[]{:S(2)}) collective-permute-start(bf16[32,3072]{1,0:T(8,128)(2,1)S(1)} %pad_maximum_fusion.3), channel_id=1, source_target_pairs={{0,14},{1,3},{2,4},{3,1},{4,2},{5,7},{6,8},{7,5},{8,6},{9,11},{10,... | collective-permute-start | bytes 589832 | tf_op jit(solution)/shard_map/ppermute | solution.py:45
  15.7 10.7 %copy-start = (bf16[768,1536]{1,0:T(8,128)(2,1)S(1)}, bf16[768,1536]{1,0:T(8,128)(2,1)}, u32[]{:S(2)}) copy-start(bf16[768,1536]{1,0:T(8,128)(2,1)} %param.6) | copy-start | bytes 7077892
  22.5 14.6 %collective-permute-start.6 = (bf16[32,3072]{1,0:T(8,128)(2,1)S(1)}, bf16[32,3072]{1,0:T(8,128)(2,1)S(1)}, u32[]{:S(2)}, u32[]{:S(2)}) collective-permute-start(bf16[32,3072]{1,0:T(8,128)(2,1)S(1)} %collective-permute-done.1), channel_id=1, source_target_pairs={{0,18},{1,31},{2,16},{3,21},{4,22},{5,19},{6,20},{7,25},{8,26},{9,... | collective-permute-start | bytes 589832 | tf_op jit(solution)/shard_map/ppermute | solution.py:45
  22.5 8.0 %collective-permute-start.4 = (bf16[32,3072]{1,0:T(8,128)(2,1)S(1)}, bf16[32,3072]{1,0:T(8,128)(2,1)S(1)}, u32[]{:S(2)}, u32[]{:S(2)}) collective-permute-start(bf16[32,3072]{1,0:T(8,128)(2,1)S(1)} %collective-permute-done.1), channel_id=1, source_target_pairs={{0,2},{1,15},{2,0},{3,5},{4,6},{5,3},{6,4},{7,9},{8,10},{9,7},{10,... | collective-permute-start | bytes 589832 | tf_op jit(solution)/shard_map/ppermute | solution.py:45
  24.5 18.4 %collective-permute-start.9 = (bf16[1536,768]{1,0:T(8,128)(2,1)}, bf16[1536,768]{1,0:T(8,128)(2,1)S(1)}, u32[]{:S(2)}, u32[]{:S(2)}) collective-permute-start(bf16[1536,768]{1,0:T(8,128)(2,1)} %param.5), channel_id=1, source_target_pairs={{0,1},{1,0},{2,3},{3,2},{4,5},{5,4},{6,7},{7,6},{8,9},{9,8},{10,11... | collective-permute-start | bytes 7077896 | tf_op jit(solution)/shard_map/ppermute | solution.py:45
  26.4 18.1 %collective-permute-start.10 = (bf16[768,1536]{1,0:T(8,128)(2,1)S(1)}, bf16[768,1536]{1,0:T(8,128)(2,1)S(1)}, u32[]{:S(2)}, u32[]{:S(2)}) collective-permute-start(bf16[768,1536]{1,0:T(8,128)(2,1)S(1)} %copy-done), channel_id=1, source_target_pairs={{0,1},{1,0},{2,3},{3,2},{4,5},{5,4},{6,7},{7,6},{8,9},{9,8},{10,11... | collective-permute-start | bytes 7077896 | tf_op jit(solution)/shard_map/ppermute | solution.py:45
  30.5 12.3 %collective-permute-start.8 = (bf16[32,3072]{1,0:T(8,128)(2,1)S(1)}, bf16[32,3072]{1,0:T(8,128)(2,1)S(1)}, u32[]{:S(2)}, u32[]{:S(2)}) collective-permute-start(bf16[32,3072]{1,0:T(8,128)(2,1)S(1)} %collective-permute-done.4), channel_id=1, source_target_pairs={{0,30},{1,19},{2,20},{3,17},{4,18},{5,23},{6,24},{7,21},{8,22},{9,... | collective-permute-start | bytes 589832 | tf_op jit(solution)/shard_map/ppermute | solution.py:45
  35.9 7.0 %collective-permute-start.7 = (bf16[32,3072]{1,0:T(8,128)(2,1)S(1)}, bf16[32,3072]{1,0:T(8,128)(2,1)S(1)}, u32[]{:S(2)}, u32[]{:S(2)}) collective-permute-start(bf16[32,3072]{1,0:T(8,128)(2,1)S(1)} %collective-permute-done.4), channel_id=1, source_target_pairs={{0,14},{1,3},{2,4},{3,1},{4,2},{5,7},{6,8},{7,5},{8,6},{9,11},{10,... | collective-permute-start | bytes 589832 | tf_op jit(solution)/shard_map/ppermute | solution.py:45
  90.3 8.8 %collective-permute-start.15 = (bf16[32,3072]{1,0:T(8,128)(2,1)S(1)}, bf16[32,3072]{1,0:T(8,128)(2,1)S(1)}, u32[]{:S(2)}, u32[]{:S(2)}) collective-permute-start(bf16[32,3072]{1,0:T(8,128)(2,1)S(1)} %pad_maximum_fusion.7), channel_id=1, source_target_pairs={{0,14},{1,3},{2,4},{3,1},{4,2},{5,7},{6,8},{7,5},{8,6},{9,11},{10,... | collective-permute-start | bytes 589832 | tf_op jit(solution)/shard_map/ppermute | solution.py:45
  92.6 9.7 %collective-permute-start.11 = (bf16[32,3072]{1,0:T(8,128)(2,1)S(1)}, bf16[32,3072]{1,0:T(8,128)(2,1)S(1)}, u32[]{:S(2)}, u32[]{:S(2)}) collective-permute-start(bf16[32,3072]{1,0:T(8,128)(2,1)S(1)} %pad_maximum_fusion.5), channel_id=1, source_target_pairs={{0,18},{1,31},{2,16},{3,21},{4,22},{5,19},{6,20},{7,25},{8,26},{9,... | collective-permute-start | bytes 589832 | tf_op jit(solution)/shard_map/ppermute | solution.py:45
  93.9 9.5 %collective-permute-start.12 = (bf16[32,3072]{1,0:T(8,128)(2,1)S(1)}, bf16[32,3072]{1,0:T(8,128)(2,1)S(1)}, u32[]{:S(2)}, u32[]{:S(2)}) collective-permute-start(bf16[32,3072]{1,0:T(8,128)(2,1)S(1)} %pad_maximum_fusion.6), channel_id=1, source_target_pairs={{0,2},{1,15},{2,0},{3,5},{4,6},{5,3},{6,4},{7,9},{8,10},{9,7},{10,... | collective-permute-start | bytes 589832 | tf_op jit(solution)/shard_map/ppermute | solution.py:45
  99.2 6.4 %collective-permute-start.16 = (bf16[32,3072]{1,0:T(8,128)(2,1)S(1)}, bf16[32,3072]{1,0:T(8,128)(2,1)S(1)}, u32[]{:S(2)}, u32[]{:S(2)}) collective-permute-start(bf16[32,3072]{1,0:T(8,128)(2,1)S(1)} %fusion.11), channel_id=1, source_target_pairs={{0,2},{1,15},{2,0},{3,5},{4,6},{5,3},{6,4},{7,9},{8,10},{9,7},{10,... | collective-permute-start | bytes 589832 | tf_op jit(solution)/shard_map/ppermute | solution.py:45
  103.5 8.4 %collective-permute-start.13 = (bf16[32,3072]{1,0:T(8,128)(2,1)S(1)}, bf16[32,3072]{1,0:T(8,128)(2,1)S(1)}, u32[]{:S(2)}, u32[]{:S(2)}) collective-permute-start(bf16[32,3072]{1,0:T(8,128)(2,1)S(1)} %fusion.10), channel_id=1, source_target_pairs={{0,14},{1,3},{2,4},{3,1},{4,2},{5,7},{6,8},{7,5},{8,6},{9,11},{10,... | collective-permute-start | bytes 589832 | tf_op jit(solution)/shard_map/ppermute | solution.py:45
  104.3 14.6 %collective-permute-start.20 = (bf16[2,256,768]{2,1,0:T(8,128)(2,1)S(1)}, bf16[2,256,768]{2,1,0:T(8,128)(2,1)S(1)}, u32[]{:S(2)}, u32[]{:S(2)}) collective-permute-start(bf16[2,256,768]{2,1,0:T(8,128)(2,1)S(1)} %pad_maximum_fusion.2), channel_id=1, source_target_pairs={{0,1},{1,0},{2,3},{3,2},{4,5},{5,4},{6,7},{7,6},{8,9},{9,8},{10,11... | collective-permute-start | bytes 2359304 | tf_op jit(solution)/shard_map/ppermute | solution.py:45
  104.3 14.6 %collective-permute-start.21 = (bf16[256,3072]{1,0:T(8,128)(2,1)S(1)}, bf16[256,3072]{1,0:T(8,128)(2,1)S(1)}, u32[]{:S(2)}, u32[]{:S(2)}) collective-permute-start(bf16[256,3072]{1,0:T(8,128)(2,1)S(1)} %constant_dynamic-update-slice_fusion.2), channel_id=1, source_target_pairs={{0,1},{1,0},{2,3},{3,2},{4,5},{5,4},{6,7},{7,6},{8,9},{9,8},{10,11... | collective-permute-start | bytes 4718600 | tf_op jit(solution)/shard_map/ppermute | solution.py:45
  105.6 8.0 %collective-permute-start.17 = (bf16[16,3072]{1,0:T(8,128)(2,1)S(1)}, bf16[16,3072]{1,0:T(8,128)(2,1)S(1)}, u32[]{:S(2)}, u32[]{:S(2)}) collective-permute-start(bf16[16,3072]{1,0:T(8,128)(2,1)S(1)} %slice.305), channel_id=1, source_target_pairs={{0,14},{1,3},{2,4},{3,1},{4,2},{5,7},{6,8},{7,5},{8,6},{9,11},{10,... | collective-permute-start | bytes 294920 | tf_op jit(solution)/shard_map/ppermute | solution.py:45
  111.9 6.8 %collective-permute-start.14 = (bf16[32,3072]{1,0:T(8,128)(2,1)S(1)}, bf16[32,3072]{1,0:T(8,128)(2,1)S(1)}, u32[]{:S(2)}, u32[]{:S(2)}) collective-permute-start(bf16[32,3072]{1,0:T(8,128)(2,1)S(1)} %fusion.9), channel_id=1, source_target_pairs={{0,2},{1,15},{2,0},{3,5},{4,6},{5,3},{6,4},{7,9},{8,10},{9,7},{10,... | collective-permute-start | bytes 589832 | tf_op jit(solution)/shard_map/ppermute | solution.py:45
  113.7 11.1 %collective-permute-start.18 = (bf16[16,3072]{1,0:T(8,128)(2,1)S(1)}, bf16[16,3072]{1,0:T(8,128)(2,1)S(1)}, u32[]{:S(2)}, u32[]{:S(2)}) collective-permute-start(bf16[16,3072]{1,0:T(8,128)(2,1)S(1)} %fusion.31), channel_id=1, source_target_pairs={{0,16},{1,17},{2,18},{3,19},{4,20},{5,21},{6,22},{7,23},{8,24},{9,... | collective-permute-start | bytes 294920 | tf_op jit(solution)/shard_map/ppermute | solution.py:45
  118.8 5.9 %collective-permute-start.19 = (bf16[16,3072]{1,0:T(8,128)(2,1)S(1)}, bf16[16,3072]{1,0:T(8,128)(2,1)S(1)}, u32[]{:S(2)}, u32[]{:S(2)}) collective-permute-start(bf16[16,3072]{1,0:T(8,128)(2,1)S(1)} %slice.304), channel_id=1, source_target_pairs={{0,14},{1,3},{2,4},{3,1},{4,2},{5,7},{6,8},{7,5},{8,6},{9,11},{10,... | collective-permute-start | bytes 294920 | tf_op jit(solution)/shard_map/ppermute | solution.py:45

commit v5 on v4

--- a/solution.py
+++ b/solution.py
@@ -56,20 +56,19 @@
     mine = jnp.concatenate([tokens, grad_out], axis=1)
     near1 = swap(mine, even[0])
     far0 = swap(mine, swap_half)
-    far1 = swap(mine, even[1])
     near01 = jnp.concatenate([mine, near1], axis=0)
     near2 = swap(near01, odd[0])
-    far2 = swap(near01, odd[1])
-    near2, far0, far1 = lax.optimization_barrier((near2, far0, far1))
+    far1 = swap(far0, even[0])
+    far01 = jnp.concatenate([far0, far1], axis=0)
     near3 = swap(near2, even[0])
-    far3 = swap(near2, even[1])
-    near3, far2 = lax.optimization_barrier((near3, far2))
+    far2 = swap(far01, odd[0])
     near4 = swap(near3, odd[0])
     far4 = swap(near3, odd[1])
-    w_up, w_down = lax.optimization_barrier((w_up, w_down, near2))[:2]
+    far3 = swap(far2, even[0])
+    w_up, w_down = lax.optimization_barrier((w_up, w_down, near3))[:2]
     w_up_all = jnp.concatenate([w_up, swap(w_up, swap_core)], axis=1)
     w_down_all = jnp.concatenate([w_down, swap(w_down, swap_core)], axis=0)
-    both = jnp.concatenate([near01, far0, far1, near2, far2, near3, far3, near4, far4], axis=0)
+    both = jnp.concatenate([near01, far01, near2, far2, near3, far3, near4, far4], axis=0)
     x_own, dy_own = both[:, :feats], both[:, feats:]
     units = both.shape[0] // rows
 

time: 126 us -> 125 us (level)
  waiting for transfers between devices: 35.5 us -> 23.4 us
  starting transfers between devices: 32.3 us -> 38.8 us
  blocking collectives: 38.4 us -> 43.8 us
    ppermute x22, waiting for transfers between devices: 35.5 us -> 23.4 us  [swap(): return lax.ppermute(value, 'col', perm)]
    ppermute x22, starting transfers between devices: 32.3 us -> 38.8 us  [swap(): return lax.ppermute(value, 'col', perm)]
    all_to_all x1, blocking collectives: 18.4 us -> 21.2 us  [local(): lax.all_to_all(jnp.broadcast_to(pair[None], (rows,) + pair.shape), 'row',...]
    all_to_all x1, blocking collectives: 20.1 us -> 22.5 us  [local(): parts = lax.all_to_all(parts, 'row', 0, 0)]
    unnamed x13 -> x15, local copies, waits for them, and re-layouts: 2.9 us -> 2.86 us
  transfers between devices with their start and end apart: 22 -> 22, of which waited for: 11 -> 8; matrix products, arithmetic and copies ran while one was open for 7% -> 6% of each run, Pallas kernels for 0% -> 0%
where the time goes in v5:
time: 125 us
  blocking collectives  43.8 us (35%)
  starting transfers between devices  38.8 us (31%)
  waiting for transfers between devices  23.4 us (19%)
  matrix products  11.7 us (9%)
  local copies, waits for them, and re-layouts  5.05 us (4%)
  other arithmetic  1.32 us (1%)
    ppermute x22, starting transfers between devices, swap(): return lax.ppermute(value, 'col', perm)  38.8 us
    ppermute x22, waiting for transfers between devices, swap(): return lax.ppermute(value, 'col', perm)  23.4 us
    all_to_all x1, blocking collectives, local(): parts = lax.all_to_all(parts, 'row', 0, 0)  22.5 us
    all_to_all x1, blocking collectives, local(): lax.all_to_all(jnp.broadcast_to(pair[None], (rows,) + pair.shape), 'row',...  21.2 us
    dot_general x2, matrix products, local(): lax.dot_general(tok[:, :feats], g, contract_first, preferred_element_type...  3.08 us
    dot_general x2, matrix products, local(): lax.dot_general(h, tok[:, feats:], contract_first, preferred_element_type...  3.03 us
    unnamed x15, local copies, waits for them, and re-layouts  2.86 us
  transfers between devices with their start and end apart: 22, of which 8 were waited for; matrix products, arithmetic and copies ran while one was open for 6% of the time, Pallas kernels for 0%

profile of v5, /device:TPU:8, one launch (start us, length us, event | category | flops | bytes accessed | tf_op | source)
XLA Modules:
  0.0 125.0 jit_solution(11511060470681954334)
XLA Ops:
  0.6 0.0 copy-start
  0.6 1.0 constant_dynamic-update-slice_fusion.1
  1.6 0.8 constant_dynamic-update-slice_fusion
  2.4 1.9 %collective-permute-start = (bf16[16,3072]{1,0:T(8,128)(2,1)S(1)}, bf16[16,3072]{1,0:T(8,128)(2,1)S(1)}, u32[]{:S(2)}, u32[]{:S(2)}) collective-permute-start(bf16[16,3072]{1,0:T(8,128)(2,1)S(1)} %get-tuple-element.47), channel_id=1, source_target_pairs={{0,2},{1,15},{2,0},{3,5},{4,6},{5,3},{6,4},{7,9},{8,10},{9,7},{10,... | collective-permute-start | bytes 294920 | tf_op jit(solution)/shard_map/ppermute | solution.py:45
  4.3 3.0 %collective-permute-start.1 = (bf16[16,3072]{1,0:T(8,128)(2,1)S(1)}, bf16[16,3072]{1,0:T(8,128)(2,1)S(1)}, u32[]{:S(2)}, u32[]{:S(2)}) collective-permute-start(bf16[16,3072]{1,0:T(8,128)(2,1)S(1)} %get-tuple-element.47), channel_id=1, source_target_pairs={{0,16},{1,17},{2,18},{3,19},{4,20},{5,21},{6,22},{7,23},{8,24},{9,... | collective-permute-start | bytes 294920 | tf_op jit(solution)/shard_map/ppermute | solution.py:45
  7.4 5.6 %collective-permute-start.3 = (bf16[32,3072]{1,0:T(8,128)(2,1)S(1)}, bf16[32,3072]{1,0:T(8,128)(2,1)S(1)}, u32[]{:S(2)}, u32[]{:S(2)}) collective-permute-start(bf16[32,3072]{1,0:T(8,128)(2,1)S(1)} %pad_maximum_fusion.3), channel_id=1, source_target_pairs={{0,14},{1,3},{2,4},{3,1},{4,2},{5,7},{6,8},{7,5},{8,6},{9,11},{10,... | collective-permute-start | bytes 589832 | tf_op jit(solution)/shard_map/ppermute | solution.py:45
  13.0 0.0 collective-permute-done.1
  13.0 4.6 %collective-permute-done.2 = bf16[16,3072]{1,0:T(8,128)(2,1)S(1)} collective-permute-done((bf16[16,3072]{1,0:T(8,128)(2,1)S(1)}, bf16[16,3072]{1,0:T(8,128)(2,1)S(1)}, u32[]{:S(2)}, u32[]{:S(2)}) %collective-permute-start.2) | collective-permute-done | bytes 98336 | tf_op jit(solution)/shard_map/ppermute | solution.py:45
  17.6 2.5 %collective-permute-start.4 = (bf16[32,3072]{1,0:T(8,128)(2,1)S(1)}, bf16[32,3072]{1,0:T(8,128)(2,1)S(1)}, u32[]{:S(2)}, u32[]{:S(2)}) collective-permute-start(bf16[32,3072]{1,0:T(8,128)(2,1)S(1)} %pad_maximum_fusion.4), channel_id=1, source_target_pairs={{0,14},{1,3},{2,4},{3,1},{4,2},{5,7},{6,8},{7,5},{8,6},{9,11},{10,... | collective-permute-start | bytes 589832 | tf_op jit(solution)/shard_map/ppermute | solution.py:45
  20.1 5.7 %collective-permute-done.5 = bf16[32,3072]{1,0:T(8,128)(2,1)S(1)} collective-permute-done((bf16[32,3072]{1,0:T(8,128)(2,1)S(1)}, bf16[32,3072]{1,0:T(8,128)(2,1)S(1)}, u32[]{:S(2)}, u32[]{:S(2)}) %collective-permute-start.5) | collective-permute-done | bytes 196640 | tf_op jit(solution)/shard_map/ppermute | solution.py:45
  25.8 0.0 collective-permute-start.9
  25.8 0.1 collective-permute-start.6
  25.9 1.1 collective-permute-start.10
  27.1 4.9 %collective-permute-start.8 = (bf16[32,3072]{1,0:T(8,128)(2,1)S(1)}, bf16[32,3072]{1,0:T(8,128)(2,1)S(1)}, u32[]{:S(2)}, u32[]{:S(2)}) collective-permute-start(bf16[32,3072]{1,0:T(8,128)(2,1)S(1)} %collective-permute-done.5), channel_id=1, source_target_pairs={{0,30},{1,19},{2,20},{3,17},{4,18},{5,23},{6,24},{7,21},{8,22},{9,... | collective-permute-start | bytes 589832 | tf_op jit(solution)/shard_map/ppermute | solution.py:45
  31.9 0.8 collective-permute-start.7
  32.8 0.0 copy-start.1
  32.8 0.2 constant_dynamic-update-slice_fusion.14
  33.0 1.5 %copy-done.1 = bf16[768,1536]{1,0:T(8,128)(2,1)S(1)} copy-done((bf16[768,1536]{1,0:T(8,128)(2,1)S(1)}, bf16[768,1536]{1,0:T(8,128)(2,1)}, u32[]{:S(2)}) %copy-start.1) | copy-done | bytes 2359320
  34.5 0.2 constant_dynamic-update-slice_fusion.16
  34.6 4.2 %collective-permute-done.7 = bf16[32,3072]{1,0:T(8,128)(2,1)S(1)} collective-permute-done((bf16[32,3072]{1,0:T(8,128)(2,1)S(1)}, bf16[32,3072]{1,0:T(8,128)(2,1)S(1)}, u32[]{:S(2)}, u32[]{:S(2)}) %collective-permute-start.7) | collective-permute-done | bytes 196640 | tf_op jit(solution)/shard_map/ppermute | solution.py:45
  38.8 0.0 collective-permute-done.8
  38.9 0.0 collective-permute-done.9
  38.9 0.2 constant_dynamic-update-slice_fusion.13
  39.1 1.4 %convolution_convert_fusion.1 = bf16[256,1536]{1,0:T(8,128)(2,1)S(1)} fusion(bf16[1536,1536]{1,0:T(8,128)(2,1)S(1)} %constant_dynamic-update-slice_fusion.13, bf16[256,3072]{1,0:T(8,128)(2,1)S(1)} %constant_dynamic-update-slice_fusion.2), kind=kOutput, calls=%fused_computation.26 | convolution fusion | flops 1208352768 | bytes 6291456 | tf_op jit(solution)/shard_map/dot_general | solution.py:75
  40.5 0.2 constant_dynamic-update-slice_fusion.15
  40.6 1.4 %convolution_convert_fusion = bf16[256,1536]{1,0:T(8,128)(2,1)S(1)} fusion(bf16[1536,1536]{1,0:T(8,128)(2,1)S(1)} %constant_dynamic-update-slice_fusion.15, bf16[256,3072]{1,0:T(8,128)(2,1)S(1)} %constant_dynamic-update-slice_fusion.2), kind=kOutput, calls=%fused_computation.25 | convolution fusion | flops 1208352768 | bytes 6291456 | tf_op jit(solution)/shard_map/dot_general | solution.py:76
  42.1 0.1 pad_maximum_fusion.1
  42.2 22.5 %all_to_all.10 = bf16[8,2,32,1536]{3,2,1,0:T(8,128)(2,1)S(1)} all-to-all(bf16[8,2,32,1536]{3,2,1,0:T(8,128)(2,1)S(1)} %pad_maximum_fusion.1), channel_id=1, replica_groups=mesh['row'=8,'col'=32] {'row'}, dimensions={0} | all-to-all | bytes 3145728 | tf_op jit(solution)/shard_map/all_to_all | solution.py:82
  64.7 0.2 convert_reduce_fusion
  65.0 0.1 multiply_convert_fusion.2
  65.1 0.1 broadcast_in_dim.2
  65.3 21.2 %all_to_all.11 = bf16[8,2,32,1536]{3,2,1,0:T(8,128)(2,1)S(1)} all-to-all(bf16[8,2,32,1536]{3,2,1,0:T(8,128)(2,1)S(1)} %broadcast_in_dim.2), channel_id=1, replica_groups=mesh['row'=8,'col'=32] {'row'}, dimensions={0} | all-to-all | bytes 3145728 | tf_op jit(solution)/shard_map/all_to_all | solution.py:86
  86.5 0.1 fusion.35
  86.7 1.4 %fusion.38 = f32[256,1536]{1,0:T(8,128)S(1)} fusion(bf16[256,1536]{1,0:T(8,128)(2,1)S(1)} %bitcast.27, bf16[1536,1536]{1,0:T(8,128)(2,1)S(1)} %constant_dynamic-update-slice_fusion.13), kind=kOutput, calls=%fused_computation.105 | convolution fusion | flops 1207959552 | bytes 7077888 | tf_op jit(solution)/shard_map/dot_general | solution.py:93
  88.1 1.4 %fusion.37 = f32[256,1536]{1,0:T(8,128)S(1)} fusion(bf16[256,1536]{1,0:T(8,128)(2,1)S(1)} %bitcast.24, bf16[1536,1536]{1,0:T(8,128)(2,1)S(1)} %constant_dynamic-update-slice_fusion.15), kind=kOutput, calls=%fused_computation.104 | convolution fusion | flops 1207959552 | bytes 7077888 | tf_op jit(solution)/shard_map/dot_general | solution.py:92
  89.5 0.2 fusion
  89.7 0.1 fusion.22
  89.8 0.8 fusion.7
  90.6 0.8 fusion.5
  91.5 2.1 %collective-permute-start.15 = (bf16[32,3072]{1,0:T(8,128)(2,1)S(1)}, bf16[32,3072]{1,0:T(8,128)(2,1)S(1)}, u32[]{:S(2)}, u32[]{:S(2)}) collective-permute-start(bf16[32,3072]{1,0:T(8,128)(2,1)S(1)} %pad_maximum_fusion.8), channel_id=1, source_target_pairs={{0,14},{1,3},{2,4},{3,1},{4,2},{5,7},{6,8},{7,5},{8,6},{9,11},{10,... | collective-permute-start | bytes 589832 | tf_op jit(solution)/shard_map/ppermute | solution.py:45
  93.7 0.1 slice_bitcast_fusion.4
  93.8 3.6 %collective-permute-start.11 = (bf16[32,3072]{1,0:T(8,128)(2,1)S(1)}, bf16[32,3072]{1,0:T(8,128)(2,1)S(1)}, u32[]{:S(2)}, u32[]{:S(2)}) collective-permute-start(bf16[32,3072]{1,0:T(8,128)(2,1)S(1)} %pad_maximum_fusion.6), channel_id=1, source_target_pairs={{0,18},{1,31},{2,16},{3,21},{4,22},{5,19},{6,20},{7,25},{8,26},{9,... | collective-permute-start | bytes 589832 | tf_op jit(solution)/shard_map/ppermute | solution.py:45
  97.4 0.0 collective-permute-start.12
  97.4 0.1 pad_maximum_fusion.2
  97.5 3.1 %collective-permute-done.15 = bf16[32,3072]{1,0:T(8,128)(2,1)S(1)} collective-permute-done((bf16[32,3072]{1,0:T(8,128)(2,1)S(1)}, bf16[32,3072]{1,0:T(8,128)(2,1)S(1)}, u32[]{:S(2)}, u32[]{:S(2)}) %collective-permute-start.15) | collective-permute-done | bytes 196640 | tf_op jit(solution)/shard_map/ppermute | solution.py:45
  100.6 1.9 %collective-permute-start.16 = (bf16[32,3072]{1,0:T(8,128)(2,1)S(1)}, bf16[32,3072]{1,0:T(8,128)(2,1)S(1)}, u32[]{:S(2)}, u32[]{:S(2)}) collective-permute-start(bf16[32,3072]{1,0:T(8,128)(2,1)S(1)} %fusion.11), channel_id=1, source_target_pairs={{0,2},{1,15},{2,0},{3,5},{4,6},{5,3},{6,4},{7,9},{8,10},{9,7},{10,... | collective-permute-start | bytes 589832 | tf_op jit(solution)/shard_map/ppermute | solution.py:45
  102.5 0.0 collective-permute-done.11
  102.5 1.1 collective-permute-done.12
  103.6 0.1 fusion.10
  103.7 2.2 %collective-permute-start.13 = (bf16[32,3072]{1,0:T(8,128)(2,1)S(1)}, bf16[32,3072]{1,0:T(8,128)(2,1)S(1)}, u32[]{:S(2)}, u32[]{:S(2)}) collective-permute-start(bf16[32,3072]{1,0:T(8,128)(2,1)S(1)} %fusion.10), channel_id=1, source_target_pairs={{0,14},{1,3},{2,4},{3,1},{4,2},{5,7},{6,8},{7,5},{8,6},{9,11},{10,... | collective-permute-start | bytes 589832 | tf_op jit(solution)/shard_map/ppermute | solution.py:45
  105.9 0.0 collective-permute-start.20
  105.9 0.5 collective-permute-start.21
  106.4 1.0 collective-permute-done.16
  107.5 2.6 %collective-permute-start.17 = (bf16[16,3072]{1,0:T(8,128)(2,1)S(1)}, bf16[16,3072]{1,0:T(8,128)(2,1)S(1)}, u32[]{:S(2)}, u32[]{:S(2)}) collective-permute-start(bf16[16,3072]{1,0:T(8,128)(2,1)S(1)} %slice.305), channel_id=1, source_target_pairs={{0,14},{1,3},{2,4},{3,1},{4,2},{5,7},{6,8},{7,5},{8,6},{9,11},{10,... | collective-permute-start | bytes 294920 | tf_op jit(solution)/shard_map/ppermute | solution.py:45
  110.0 0.6 collective-permute-done.13
  110.7 0.5 collective-permute-start.14
  111.2 3.2 %collective-permute-done.17 = bf16[16,3072]{1,0:T(8,128)(2,1)S(1)} collective-permute-done((bf16[16,3072]{1,0:T(8,128)(2,1)S(1)}, bf16[16,3072]{1,0:T(8,128)(2,1)S(1)}, u32[]{:S(2)}, u32[]{:S(2)}) %collective-permute-start.17) | collective-permute-done | bytes 98336 | tf_op jit(solution)/shard_map/ppermute | solution.py:45
  114.5 3.7 %collective-permute-start.18 = (bf16[16,3072]{1,0:T(8,128)(2,1)S(1)}, bf16[16,3072]{1,0:T(8,128)(2,1)S(1)}, u32[]{:S(2)}, u32[]{:S(2)}) collective-permute-start(bf16[16,3072]{1,0:T(8,128)(2,1)S(1)} %fusion.31), channel_id=1, source_target_pairs={{0,16},{1,17},{2,18},{3,19},{4,20},{5,21},{6,22},{7,23},{8,24},{9,... | collective-permute-start | bytes 294920 | tf_op jit(solution)/shard_map/ppermute | solution.py:45
  118.3 1.6 %collective-permute-start.19 = (bf16[16,3072]{1,0:T(8,128)(2,1)S(1)}, bf16[16,3072]{1,0:T(8,128)(2,1)S(1)}, u32[]{:S(2)}, u32[]{:S(2)}) collective-permute-start(bf16[16,3072]{1,0:T(8,128)(2,1)S(1)} %slice.304), channel_id=1, source_target_pairs={{0,14},{1,3},{2,4},{3,1},{4,2},{5,7},{6,8},{7,5},{8,6},{9,11},{10,... | collective-permute-start | bytes 294920 | tf_op jit(solution)/shard_map/ppermute | solution.py:45
  119.9 0.0 collective-permute-done.20
  119.9 0.0 collective-permute-done.21
  119.9 2.2 %multiply_convert_fusion.1 = bf16[768,1536]{1,0:T(8,128)(2,1)} fusion(f32[768,1536]{1,0:T(8,128)S(1)} %fusion.7, bf16[256,3072]{1,0:T(8,128)(2,1)S(1)} %collective-permute-done.21, bf16[2,256,768]{2,1,0:T(8,128)(2,1)S(1)} %collective-permute-done.20), kind=kOutput, calls=%fused_computation.22 | convolution fusion | flops 607518720 | bytes 8257536 | tf_op jit(solution)/shard_map/dot_general | solution.py:123
  122.1 2.2 %multiply_convert_fusion = bf16[1536,768]{1,0:T(8,128)(2,1)} fusion(f32[1536,768]{1,0:T(8,128)S(1)} %fusion.5, bf16[256,3072]{1,0:T(8,128)(2,1)S(1)} %collective-permute-done.21, bf16[2,256,768]{2,1,0:T(8,128)(2,1)S(1)} %collective-permute-done.20), kind=kOutput, calls=%fused_computation.21 | convolution fusion | flops 607518720 | bytes 8257536 | tf_op jit(solution)/shard_map/dot_general | solution.py:120
  124.4 0.6 fusion.36
  (36 shorter events, 0.6 us)
Async XLA Ops:
  0.6 32.2 %copy-start = (bf16[1536,768]{1,0:T(8,128)(2,1)S(1)}, bf16[1536,768]{1,0:T(8,128)(2,1)}, u32[]{:S(2)}) copy-start(bf16[1536,768]{1,0:T(8,128)(2,1)} %param.5) | copy-start | bytes 7077892
  2.4 4.9 %collective-permute-start = (bf16[16,3072]{1,0:T(8,128)(2,1)S(1)}, bf16[16,3072]{1,0:T(8,128)(2,1)S(1)}, u32[]{:S(2)}, u32[]{:S(2)}) collective-permute-start(bf16[16,3072]{1,0:T(8,128)(2,1)S(1)} %get-tuple-element.47), channel_id=1, source_target_pairs={{0,2},{1,15},{2,0},{3,5},{4,6},{5,3},{6,4},{7,9},{8,10},{9,7},{10,... | collective-permute-start | bytes 294920 | tf_op jit(solution)/shard_map/ppermute | solution.py:45
  4.3 8.7 %collective-permute-start.1 = (bf16[16,3072]{1,0:T(8,128)(2,1)S(1)}, bf16[16,3072]{1,0:T(8,128)(2,1)S(1)}, u32[]{:S(2)}, u32[]{:S(2)}) collective-permute-start(bf16[16,3072]{1,0:T(8,128)(2,1)S(1)} %get-tuple-element.47), channel_id=1, source_target_pairs={{0,16},{1,17},{2,18},{3,19},{4,20},{5,21},{6,22},{7,23},{8,24},{9,... | collective-permute-start | bytes 294920 | tf_op jit(solution)/shard_map/ppermute | solution.py:45
  7.4 12.7 %collective-permute-start.3 = (bf16[32,3072]{1,0:T(8,128)(2,1)S(1)}, bf16[32,3072]{1,0:T(8,128)(2,1)S(1)}, u32[]{:S(2)}, u32[]{:S(2)}) collective-permute-start(bf16[32,3072]{1,0:T(8,128)(2,1)S(1)} %pad_maximum_fusion.3), channel_id=1, source_target_pairs={{0,14},{1,3},{2,4},{3,1},{4,2},{5,7},{6,8},{7,5},{8,6},{9,11},{10,... | collective-permute-start | bytes 589832 | tf_op jit(solution)/shard_map/ppermute | solution.py:45
  13.0 4.6 %collective-permute-start.2 = (bf16[16,3072]{1,0:T(8,128)(2,1)S(1)}, bf16[16,3072]{1,0:T(8,128)(2,1)S(1)}, u32[]{:S(2)}, u32[]{:S(2)}) collective-permute-start(bf16[16,3072]{1,0:T(8,128)(2,1)S(1)} %collective-permute-done.1), channel_id=1, source_target_pairs={{0,2},{1,15},{2,0},{3,5},{4,6},{5,3},{6,4},{7,9},{8,10},{9,7},{10,... | collective-permute-start | bytes 294920 | tf_op jit(solution)/shard_map/ppermute | solution.py:45
  17.6 8.2 %collective-permute-start.4 = (bf16[32,3072]{1,0:T(8,128)(2,1)S(1)}, bf16[32,3072]{1,0:T(8,128)(2,1)S(1)}, u32[]{:S(2)}, u32[]{:S(2)}) collective-permute-start(bf16[32,3072]{1,0:T(8,128)(2,1)S(1)} %pad_maximum_fusion.4), channel_id=1, source_target_pairs={{0,14},{1,3},{2,4},{3,1},{4,2},{5,7},{6,8},{7,5},{8,6},{9,11},{10,... | collective-permute-start | bytes 589832 | tf_op jit(solution)/shard_map/ppermute | solution.py:45
  20.1 5.7 %collective-permute-start.5 = (bf16[32,3072]{1,0:T(8,128)(2,1)S(1)}, bf16[32,3072]{1,0:T(8,128)(2,1)S(1)}, u32[]{:S(2)}, u32[]{:S(2)}) collective-permute-start(bf16[32,3072]{1,0:T(8,128)(2,1)S(1)} %collective-permute-done.3), channel_id=1, source_target_pairs={{0,2},{1,15},{2,0},{3,5},{4,6},{5,3},{6,4},{7,9},{8,10},{9,7},{10,... | collective-permute-start | bytes 589832 | tf_op jit(solution)/shard_map/ppermute | solution.py:45
  25.8 13.1 %collective-permute-start.9 = (bf16[1536,768]{1,0:T(8,128)(2,1)}, bf16[1536,768]{1,0:T(8,128)(2,1)S(1)}, u32[]{:S(2)}, u32[]{:S(2)}) collective-permute-start(bf16[1536,768]{1,0:T(8,128)(2,1)} %param.5), channel_id=1, source_target_pairs={{0,1},{1,0},{2,3},{3,2},{4,5},{5,4},{6,7},{7,6},{8,9},{9,8},{10,11... | collective-permute-start | bytes 7077896 | tf_op jit(solution)/shard_map/ppermute | solution.py:45
  25.8 8.8 %collective-permute-start.6 = (bf16[32,3072]{1,0:T(8,128)(2,1)S(1)}, bf16[32,3072]{1,0:T(8,128)(2,1)S(1)}, u32[]{:S(2)}, u32[]{:S(2)}) collective-permute-start(bf16[32,3072]{1,0:T(8,128)(2,1)S(1)} %collective-permute-done.4), channel_id=1, source_target_pairs={{0,2},{1,15},{2,0},{3,5},{4,6},{5,3},{6,4},{7,9},{8,10},{9,7},{10,... | collective-permute-start | bytes 589832 | tf_op jit(solution)/shard_map/ppermute | solution.py:45
  25.9 14.5 %collective-permute-start.10 = (bf16[768,1536]{1,0:T(8,128)(2,1)}, bf16[768,1536]{1,0:T(8,128)(2,1)S(1)}, u32[]{:S(2)}, u32[]{:S(2)}) collective-permute-start(bf16[768,1536]{1,0:T(8,128)(2,1)} %param.6), channel_id=1, source_target_pairs={{0,1},{1,0},{2,3},{3,2},{4,5},{5,4},{6,7},{7,6},{8,9},{9,8},{10,11... | collective-permute-start | bytes 7077896 | tf_op jit(solution)/shard_map/ppermute | solution.py:45
  27.1 11.8 %collective-permute-start.8 = (bf16[32,3072]{1,0:T(8,128)(2,1)S(1)}, bf16[32,3072]{1,0:T(8,128)(2,1)S(1)}, u32[]{:S(2)}, u32[]{:S(2)}) collective-permute-start(bf16[32,3072]{1,0:T(8,128)(2,1)S(1)} %collective-permute-done.5), channel_id=1, source_target_pairs={{0,30},{1,19},{2,20},{3,17},{4,18},{5,23},{6,24},{7,21},{8,22},{9,... | collective-permute-start | bytes 589832 | tf_op jit(solution)/shard_map/ppermute | solution.py:45
  31.9 6.9 %collective-permute-start.7 = (bf16[32,3072]{1,0:T(8,128)(2,1)S(1)}, bf16[32,3072]{1,0:T(8,128)(2,1)S(1)}, u32[]{:S(2)}, u32[]{:S(2)}) collective-permute-start(bf16[32,3072]{1,0:T(8,128)(2,1)S(1)} %collective-permute-done.5), channel_id=1, source_target_pairs={{0,14},{1,3},{2,4},{3,1},{4,2},{5,7},{6,8},{7,5},{8,6},{9,11},{10,... | collective-permute-start | bytes 589832 | tf_op jit(solution)/shard_map/ppermute | solution.py:45
  32.8 1.7 %copy-start.1 = (bf16[768,1536]{1,0:T(8,128)(2,1)S(1)}, bf16[768,1536]{1,0:T(8,128)(2,1)}, u32[]{:S(2)}) copy-start(bf16[768,1536]{1,0:T(8,128)(2,1)} %param.6) | copy-start | bytes 7077892
  91.5 9.0 %collective-permute-start.15 = (bf16[32,3072]{1,0:T(8,128)(2,1)S(1)}, bf16[32,3072]{1,0:T(8,128)(2,1)S(1)}, u32[]{:S(2)}, u32[]{:S(2)}) collective-permute-start(bf16[32,3072]{1,0:T(8,128)(2,1)S(1)} %pad_maximum_fusion.8), channel_id=1, source_target_pairs={{0,14},{1,3},{2,4},{3,1},{4,2},{5,7},{6,8},{7,5},{8,6},{9,11},{10,... | collective-permute-start | bytes 589832 | tf_op jit(solution)/shard_map/ppermute | solution.py:45
  93.8 8.8 %collective-permute-start.11 = (bf16[32,3072]{1,0:T(8,128)(2,1)S(1)}, bf16[32,3072]{1,0:T(8,128)(2,1)S(1)}, u32[]{:S(2)}, u32[]{:S(2)}) collective-permute-start(bf16[32,3072]{1,0:T(8,128)(2,1)S(1)} %pad_maximum_fusion.6), channel_id=1, source_target_pairs={{0,18},{1,31},{2,16},{3,21},{4,22},{5,19},{6,20},{7,25},{8,26},{9,... | collective-permute-start | bytes 589832 | tf_op jit(solution)/shard_map/ppermute | solution.py:45
  97.4 6.2 %collective-permute-start.12 = (bf16[32,3072]{1,0:T(8,128)(2,1)S(1)}, bf16[32,3072]{1,0:T(8,128)(2,1)S(1)}, u32[]{:S(2)}, u32[]{:S(2)}) collective-permute-start(bf16[32,3072]{1,0:T(8,128)(2,1)S(1)} %pad_maximum_fusion.7), channel_id=1, source_target_pairs={{0,2},{1,15},{2,0},{3,5},{4,6},{5,3},{6,4},{7,9},{8,10},{9,7},{10,... | collective-permute-start | bytes 589832 | tf_op jit(solution)/shard_map/ppermute | solution.py:45
  100.6 6.8 %collective-permute-start.16 = (bf16[32,3072]{1,0:T(8,128)(2,1)S(1)}, bf16[32,3072]{1,0:T(8,128)(2,1)S(1)}, u32[]{:S(2)}, u32[]{:S(2)}) collective-permute-start(bf16[32,3072]{1,0:T(8,128)(2,1)S(1)} %fusion.11), channel_id=1, source_target_pairs={{0,2},{1,15},{2,0},{3,5},{4,6},{5,3},{6,4},{7,9},{8,10},{9,7},{10,... | collective-permute-start | bytes 589832 | tf_op jit(solution)/shard_map/ppermute | solution.py:45
  103.7 7.0 %collective-permute-start.13 = (bf16[32,3072]{1,0:T(8,128)(2,1)S(1)}, bf16[32,3072]{1,0:T(8,128)(2,1)S(1)}, u32[]{:S(2)}, u32[]{:S(2)}) collective-permute-start(bf16[32,3072]{1,0:T(8,128)(2,1)S(1)} %fusion.10), channel_id=1, source_target_pairs={{0,14},{1,3},{2,4},{3,1},{4,2},{5,7},{6,8},{7,5},{8,6},{9,11},{10,... | collective-permute-start | bytes 589832 | tf_op jit(solution)/shard_map/ppermute | solution.py:45
  105.9 14.0 %collective-permute-start.20 = (bf16[2,256,768]{2,1,0:T(8,128)(2,1)S(1)}, bf16[2,256,768]{2,1,0:T(8,128)(2,1)S(1)}, u32[]{:S(2)}, u32[]{:S(2)}) collective-permute-start(bf16[2,256,768]{2,1,0:T(8,128)(2,1)S(1)} %pad_maximum_fusion.2), channel_id=1, source_target_pairs={{0,1},{1,0},{2,3},{3,2},{4,5},{5,4},{6,7},{7,6},{8,9},{9,8},{10,11... | collective-permute-start | bytes 2359304 | tf_op jit(solution)/shard_map/ppermute | solution.py:45
  105.9 14.0 %collective-permute-start.21 = (bf16[256,3072]{1,0:T(8,128)(2,1)S(1)}, bf16[256,3072]{1,0:T(8,128)(2,1)S(1)}, u32[]{:S(2)}, u32[]{:S(2)}) collective-permute-start(bf16[256,3072]{1,0:T(8,128)(2,1)S(1)} %constant_dynamic-update-slice_fusion.2), channel_id=1, source_target_pairs={{0,1},{1,0},{2,3},{3,2},{4,5},{5,4},{6,7},{7,6},{8,9},{9,8},{10,11... | collective-permute-start | bytes 4718600 | tf_op jit(solution)/shard_map/ppermute | solution.py:45
  107.5 7.0 %collective-permute-start.17 = (bf16[16,3072]{1,0:T(8,128)(2,1)S(1)}, bf16[16,3072]{1,0:T(8,128)(2,1)S(1)}, u32[]{:S(2)}, u32[]{:S(2)}) collective-permute-start(bf16[16,3072]{1,0:T(8,128)(2,1)S(1)} %slice.305), channel_id=1, source_target_pairs={{0,14},{1,3},{2,4},{3,1},{4,2},{5,7},{6,8},{7,5},{8,6},{9,11},{10,... | collective-permute-start | bytes 294920 | tf_op jit(solution)/shard_map/ppermute | solution.py:45
  110.7 7.5 %collective-permute-start.14 = (bf16[32,3072]{1,0:T(8,128)(2,1)S(1)}, bf16[32,3072]{1,0:T(8,128)(2,1)S(1)}, u32[]{:S(2)}, u32[]{:S(2)}) collective-permute-start(bf16[32,3072]{1,0:T(8,128)(2,1)S(1)} %fusion.9), channel_id=1, source_target_pairs={{0,2},{1,15},{2,0},{3,5},{4,6},{5,3},{6,4},{7,9},{8,10},{9,7},{10,... | collective-permute-start | bytes 589832 | tf_op jit(solution)/shard_map/ppermute | solution.py:45
  114.5 9.9 %collective-permute-start.18 = (bf16[16,3072]{1,0:T(8,128)(2,1)S(1)}, bf16[16,3072]{1,0:T(8,128)(2,1)S(1)}, u32[]{:S(2)}, u32[]{:S(2)}) collective-permute-start(bf16[16,3072]{1,0:T(8,128)(2,1)S(1)} %fusion.31), channel_id=1, source_target_pairs={{0,16},{1,17},{2,18},{3,19},{4,20},{5,21},{6,22},{7,23},{8,24},{9,... | collective-permute-start | bytes 294920 | tf_op jit(solution)/shard_map/ppermute | solution.py:45
  118.3 6.1 %collective-permute-start.19 = (bf16[16,3072]{1,0:T(8,128)(2,1)S(1)}, bf16[16,3072]{1,0:T(8,128)(2,1)S(1)}, u32[]{:S(2)}, u32[]{:S(2)}) collective-permute-start(bf16[16,3072]{1,0:T(8,128)(2,1)S(1)} %slice.304), channel_id=1, source_target_pairs={{0,14},{1,3},{2,4},{3,1},{4,2},{5,7},{6,8},{7,5},{8,6},{9,11},{10,... | collective-permute-start | bytes 294920 | tf_op jit(solution)/shard_map/ppermute | solution.py:45
